TPU v7x, 128 devices: a whole 4x4x4 slice. The times are simulated.
128 devices in a mesh: tile: 32 (over y, z, core), net: 4 (over x).
Axes of the slice: x: 4, y: 4, z: 4, core: 2. Of those that a mesh axis runs over, the one named last changes fastest.
Arguments:
- seg_start: float32 [16384, 128], P(('tile', 'net')), may hold values from 0 to 8
- seg_len: float32 [16384, 128], P(('tile', 'net')), may hold values from 0.25 to 2
- seg_track: float32 [16384, 128], P(('tile', 'net')), may hold values from -1 to 1
- seg_nbr: int32 [16384, 4], P(('tile', 'net')), may hold values from 0 to 16383, as said below
- seg_owner: int32 [16384, 128, 1], P(('tile', 'net')), may hold values from 0 to 127; in each aligned block of 16384 rows (0 to 16383, 16384 to 32767, ..., all dimensions but the last counted through in order) at most 256 rows name the same one
- seg_local: int32 [16384, 128], P(('tile', 'net')), may hold values from 0 to 511
- seg_node: int32 [16384, 128], P(('tile', 'net')), may hold values from 0 to 31
- pin_res: float32 [32, 65536], P(None, ('tile', 'net')), may hold values from 0.02 to 0.2
- load_cap: float32 [32, 65536], P(None, ('tile', 'net')), may hold values from 0.1 to 1
- crit_weight: float32 [32, 65536], P(None, ('tile', 'net')), may hold values from 0.1 to 1
- net_parent: int32 [32, 65536], P(None, ('tile', 'net')), may hold values from -1 to 30, as said below
Outputs:
- seg_cap: float32 [16384, 128], P(('tile', 'net'))
- delay: float32 [32, 65536], P(None, ('tile', 'net'))
- seg_sens: float32 [16384, 128], P(('tile', 'net'))
Inputs may be any that keep to these rules, and one draw needn't show every extreme that they name: `seg_nbr`: each listed block is another block within 4 blocks of the listing block; the first listed block of every block lies exactly 4 blocks away. `seg_owner`: among the segments of one device at most 256 name any one owner, and in some device one owner is named exactly 256 times. `net_parent`: node 0 of each net has parent -1; every other node's parent has a smaller index.
All inputs are finite; a program needn't handle non-finite values.
Results may differ from a plain program's by a relative error of at most 0.0003.
Values sent between devices are 32-bit elements; how exact they have to be, the bound alone decides.
No kernel may reach another device: no remote copies, remote signals or barrier semaphores. Data moves between devices by JAX's collectives and lax.ppermute only.
A program may use at most 128 MiB of HBM per device.

v0:
```python
import math

import jax
import jax.numpy as jnp
from jax import lax
from jax.sharding import PartitionSpec as P

RIM = 4


GROUND = 0.2
COUPLE = 0.005
SHEET = 0.02
HIGHEST = lax.Precision.HIGHEST


def extended(block, sides, width):
    for axis, dim in sides:
        count = lax.axis_size(axis)
        forward = [(i, i + 1) for i in range(count - 1)]
        backward = [(target, source) for source, target in forward]
        low = lax.ppermute(
            lax.slice_in_dim(block, block.shape[dim] - width, None, axis=dim), axis, forward
        )
        high = lax.ppermute(lax.slice_in_dim(block, 0, width, axis=dim), axis, backward)
        block = jnp.concatenate([low, block, high], axis=dim)
    return block


def couple(own_feats, near_feats):
    start_i = own_feats[:, 0, :, None]
    end_i = start_i + own_feats[:, 1, :, None]
    track_i = own_feats[:, 2, :, None]
    start_j = near_feats[:, 0, None, :]
    end_j = start_j + near_feats[:, 1, None, :]
    track_j = near_feats[:, 2, None, :]
    common_len = jnp.maximum(jnp.minimum(end_i, end_j) - jnp.maximum(start_i, start_j), 0.0)
    return COUPLE * jnp.sum(common_len * jnp.exp(-jnp.abs(track_i - track_j)), axis=2)


def matmul_batch(left, right):
    return jnp.einsum("ijn,jkn->ikn", left, right, precision=lax.Precision.HIGHEST)


def elmore(parent_of, node_cap, node_res, weight):
    node_count = parent_of.shape[0]
    node_index = jnp.arange(node_count, dtype=jnp.int32)
    step_mat = (parent_of[None, :, :] == node_index[:, None, None]).astype(jnp.float32)
    identity = (node_index[:, None] == node_index[None, :]).astype(jnp.float32)[:, :, None]
    path_mat = identity + step_mat
    power_mat = step_mat
    for level in range(node_count.bit_length() - 2):
        power_mat = matmul_batch(power_mat, power_mat)
        path_mat = path_mat + matmul_batch(path_mat, power_mat)
    subtree = jnp.einsum("akn,kn->an", path_mat, node_cap, precision=HIGHEST)
    delay = jnp.einsum("akn,an->kn", path_mat, node_res * subtree, precision=HIGHEST)
    below = jnp.einsum("akn,kn->an", path_mat, weight, precision=HIGHEST)
    grad_cap = jnp.einsum("akn,an->kn", path_mat, node_res * below, precision=HIGHEST)
    grad_res = below * subtree
    return (delay, grad_cap, grad_res)


def deliver(outbox):
    return lax.all_to_all(outbox, ("tile", "net"), split_axis=0, concat_axis=0, tiled=True)


def give_back(reply):
    return lax.all_to_all(reply, ("tile", "net"), split_axis=0, concat_axis=0, tiled=True)


def body(
    seg_start,
    seg_len,
    seg_track,
    seg_nbr,
    seg_owner,
    seg_local,
    seg_node,
    pin_res,
    load_cap,
    crit_weight,
    net_parent,
):
    block_count = seg_start.shape[0]
    tiles = lax.axis_size("tile")
    shards = lax.axis_size("net")
    devices = tiles * shards
    rim_width = RIM
    feats = jnp.stack([seg_start, seg_len, seg_track], axis=1)
    padded = extended(feats, ((("tile", "net"), 0),), rim_width)
    first_block = lax.axis_index(("tile", "net")) * block_count
    group_size = math.gcd(block_count, 64)
    group_rows = jnp.arange(group_size, dtype=jnp.int32)

    def one_group(index):
        first_row = index * group_size
        own_feats = lax.dynamic_slice_in_dim(feats, first_row, group_size, 0)
        own_nbr = lax.dynamic_slice_in_dim(seg_nbr, first_row, group_size, 0)
        windows = [
            lax.dynamic_slice_in_dim(padded, first_row + rim_width + offset, group_size, 0)
            for offset in range(-rim_width, rim_width + 1)
        ]
        block_ids = first_block + first_row + group_rows
        running = jnp.zeros((group_size, 128), jnp.float32)
        for neighbour in range(own_nbr.shape[1]):
            relative = own_nbr[:, neighbour] - block_ids
            near = windows[0]
            for position in range(1, 2 * rim_width + 1):
                near = jnp.where(
                    (relative == position - rim_width)[:, None, None], windows[position], near
                )
            running = running + couple(own_feats, near)
        return running

    coupling = lax.map(one_group, jnp.arange(block_count // group_size, dtype=jnp.int32)).reshape(
        block_count, 128
    )
    seg_cap = GROUND * seg_len + coupling
    owner_of = seg_owner[:, :, 0]
    row_index = jnp.arange(128, dtype=jnp.int32)
    lower_tri = (row_index[:, None] >= row_index[None, :]).astype(jnp.bfloat16)
    owner_ids = jnp.arange(devices, dtype=jnp.int32)

    def rank_step(carried, owner_group):
        hits = (owner_group[:, :, None] == owner_ids).astype(jnp.bfloat16)
        inside = jnp.einsum("ij,gjd->gid", lower_tri, hits, preferred_element_type=jnp.float32)
        totals = inside[:, -1, :]
        before = jnp.cumsum(totals, axis=0) - totals + carried[None, :]
        placed = jnp.sum((inside + before[:, None, :]) * hits, axis=2) - 1.0
        return (carried + jnp.sum(totals, axis=0), placed.astype(jnp.int32))

    owner_groups = owner_of.reshape(block_count // group_size, group_size, 128)
    unused, rank_of = lax.scan(rank_step, jnp.zeros((devices,), jnp.float32), owner_groups)
    node_count, net_count = pin_res.shape
    capacity = 2 * block_count * 128 // devices
    owner_flat = owner_of.reshape(-1)
    rank_flat = rank_of.reshape(-1)
    slot_value = (seg_node * net_count + seg_local).astype(jnp.float32)
    payload = jnp.stack([seg_cap, SHEET * seg_len, slot_value], axis=-1).reshape(-1, 3)
    outbox = (
        jnp.zeros((devices, 3, capacity), jnp.float32).at[owner_flat, :, rank_flat].set(payload)
    )
    inbox = deliver(outbox)
    slot_flat = inbox[:, 2, :].astype(jnp.int32).reshape(-1)
    slot_total = node_count * net_count
    cap_sum = jax.ops.segment_sum(inbox[:, 0, :].reshape(-1), slot_flat, slot_total)
    res_sum = jax.ops.segment_sum(inbox[:, 1, :].reshape(-1), slot_flat, slot_total)
    node_cap = load_cap + cap_sum.reshape(node_count, net_count)
    node_res = pin_res + res_sum.reshape(node_count, net_count)
    delay, grad_cap, grad_res = elmore(net_parent, node_cap, node_res, crit_weight)
    node_sens = (SHEET * grad_res + GROUND * grad_cap).reshape(-1)
    picked = node_sens[slot_flat]
    reply = picked.reshape(devices, 1, capacity)
    returned = give_back(reply)
    returned_rows = returned[:, 0, :]
    seg_sens = returned_rows[owner_flat, rank_flat]
    return (seg_cap, delay, seg_sens.reshape(block_count, 128))


def solution(mesh):
    placed = (
        P(("tile", "net"), None),
        P(("tile", "net"), None),
        P(("tile", "net"), None),
        P(("tile", "net"), None),
        P(("tile", "net"), None, None),
        P(("tile", "net"), None),
        P(("tile", "net"), None),
        P(None, ("tile", "net")),
        P(None, ("tile", "net")),
        P(None, ("tile", "net")),
        P(None, ("tile", "net")),
    )
    return jax.shard_map(
        body,
        mesh=mesh,
        in_specs=placed,
        out_specs=(P(("tile", "net"), None), P(None, ("tile", "net")), P(("tile", "net"), None)),
        check_vma=False,
    )
```

profile of v0, /device:TPU:1, one launch (start us, length us, event | category | flops | bytes accessed | tf_op | source)
XLA Modules:
  0.0 1216.1 jit_solution(2767150804011167093)
XLA Ops:
  1.6 3.9 collective-permute-start
  9.3 9.9 while.31
  21.1 10.5 fusion.36
  31.6 11.1 fusion.30
  42.7 11.1 fusion.32
  53.8 11.1 fusion.26
  64.9 18.1 %bitcast_add_fusion.2 = f32[32,32,512]{0,1,2:T(8,128)} fusion(f32[512,32,32]{2,1,0:T(8,128)} %fusion.32, f32[512,32,32]{2,1,0:T(8,128)S(1)} %fusion.30, s32[32,512]{0,1:T(8,128)S(1)} %copy.53, f32[32,32]{0,1:T(8,128)S(1)} %fusion.56), kind=kOutput, calls=%fused_computation.99 | convolution fusion | flops 206045184 | bytes 6361088 | tf_op jit(solution)/shard_map/ijn,jkn->ikn/dot_general | solution.py:42
  83.1 15.9 %bitcast_add_fusion.1 = f32[32,32,512]{0,1,2:T(8,128)} fusion(f32[32,32,512]{0,1,2:T(8,128)} %bitcast_add_fusion.2, f32[512,32,32]{2,1,0:T(8,128)S(1)} %fusion.26), kind=kOutput, calls=%fused_computation.94 | convolution fusion | flops 201850880 | bytes 6291456 | tf_op jit(solution)/shard_map/ijn,jkn->ikn/dot_general | solution.py:42
  99.3 31.3 %while.30 = (s32[]{:T(128)}, f32[2,64,128]{2,1,0:T(8,128)S(1)}, s32[2]{0:T(128)S(1)}, f32[128,3,128]{2,0,1:T(8,128)S(1)}, s32[128,4]{0,1:T(4,128)S(1)}, /*index=...) while((s32[]{:T(128)}, f32[2,64,128]{2,1,0:T(8,128)S(1)}, ...), condition=%wide.region_5.6_spmd.clone, body=%wide.region_0.5_spmd.clone.sunk | while | flops 38578536 | bytes 5744536 | solution.py:115
  101.5 13.5 %multiply_reduce_fusion.12 = (f32[64,128]{1,0:T(8,128)S(1)}, f32[64,128]{1,0:T(8,128)S(1)}, f32[64,128]{1,0:T(8,128)S(1)}, f32[64,128]{1,0:T(8,128)S(1)}) fusion(f32[64,128]{1,0:T(8,128)S(1)} %get-tuple-element.536, f32[64,128]{1,0:T(8,128)S(1)} %get-tuple-element.537, f32[64,128]{1,0:T(8,128)S(1)} %get-tuple-element.538, ...), kind=kLoop, calls=%fused_computation.10.clone.1 | loop fusion | flops 37715968 | bytes 622592 | tf_op jit(solution)/shard_map/while/body/eval_jaxpr/reduce_sum | solution.py:38
  117.1 13.5 %multiply_reduce_fusion.12 = (f32[64,128]{1,0:T(8,128)S(1)}, f32[64,128]{1,0:T(8,128)S(1)}, f32[64,128]{1,0:T(8,128)S(1)}, f32[64,128]{1,0:T(8,128)S(1)}) fusion(f32[64,128]{1,0:T(8,128)S(1)} %get-tuple-element.536, f32[64,128]{1,0:T(8,128)S(1)} %get-tuple-element.537, f32[64,128]{1,0:T(8,128)S(1)} %get-tuple-element.538, ...), kind=kLoop, calls=%fused_computation.10.clone.1 | loop fusion | flops 37715968 | bytes 622592 | tf_op jit(solution)/shard_map/while/body/eval_jaxpr/reduce_sum | solution.py:38
  130.9 5.0 copy.51
  135.9 47.4 %scatter_custom_fusion.2 = f32[3,32768]{0,1:T(8,128)} fusion(s32[16384]{0:T(1024)S(1)} %broadcast_select_fusion.1, f32[16384,3]{1,0:T(8,128)} %copy.51, f32[]{:T(128)} %constant.224.clone.1), kind=kCustom, calls=%fused_computation.113 | custom fusion | bytes 393728
  183.3 9.9 copy.52
  193.1 9.9 all-to-all-start
  203.1 16.6 %fusion.22 = f32[512,32,32]{2,1,0:T(8,128)} fusion(f32[512,32,32]{2,1,0:T(8,128)} %copy-done), kind=kOutput, calls=%fused_computation.95 | convolution fusion | flops 201326592 | bytes 4194304 | tf_op jit(solution)/shard_map/ijn,jkn->ikn/dot_general | solution.py:42
  220.0 204.2 %scatter_custom_fusion = f32[16384]{0:T(1024)S(1)} fusion(s32[32768]{0:T(1024)S(1)} %bitcast.203, f32[32768]{0:T(1024)S(1)} %bitcast.214, f32[]{:T(128)} %constant.224.clone.1), kind=kCustom, calls=%fused_computation.151 | custom fusion | flops 32768 | bytes 65540 | tf_op jit(solution)/shard_map/scatter-add | solution.py:147
  424.2 204.2 %scatter_custom_fusion.1 = f32[16384]{0:T(1024)S(1)} fusion(s32[32768]{0:T(1024)S(1)} %bitcast.204, f32[32768]{0:T(1024)S(1)} %bitcast.213, f32[]{:T(128)} %constant.224.clone.1), kind=kCustom, calls=%fused_computation.149 | custom fusion | flops 32768 | bytes 65540 | tf_op jit(solution)/shard_map/scatter-add | solution.py:146
  628.8 20.3 %multiply_reduce_fusion.6 = (f32[512,32]{1,0:T(8,128)S(1)}, f32[512,32]{1,0:T(8,128)S(1)}, f32[32,32,512]{0,1,2:T(8,128)}) fusion(f32[512,32]{1,0:T(8,128)S(1)} %copy.97, f32[512,32]{1,0:T(8,128)S(1)} %copy.95, f32[32,32,512]{0,1,2:T(8,128)} %bitcast_add_fusion.1, f32[512,32,32]{2,1,0:T(8,128)} %fusion.22), kind=kOutput, calls=%fused_computation.110 | convolution fusion | flops 203915264 | bytes 6553600 | tf_op jit(solution)/shard_map/ijn,jkn->ikn/dot_general | solution.py:42
  649.7 6.7 multiply_reduce_fusion.5
  656.5 320.1 %gather_fusion = f32[32768]{0:T(1024)} fusion(f32[16384]{0:T(1024)S(1)} %bitcast.193, s32[32768]{0:T(1024)S(1)} %broadcast_clamp_fusion), kind=kCustom, calls=%fused_computation | custom fusion | bytes 393216 | tf_op jit(solution)/shard_map/gather | solution.py:152
  976.6 29.6 %all-to-all-start.1 = ((f32[128,1,256]{2,1,0:T(1,128)}), f32[128,1,256]{2,1,0:T(1,128)S(1)}, u32[]{:S(2)}, u32[]{:S(2)}) async-start(f32[128,1,256]{2,1,0:T(1,128)} %bitcast.37), calls=%async_computation.1 | async-start | bytes 262144 | tf_op jit(solution)/shard_map/all_to_all | solution.py:68
  1006.9 9.3 all-to-all-done.1
  1016.3 199.6 %gather_fusion.1 = f32[16384]{0:T(1024)} fusion(f32[128,256]{1,0:T(8,128)S(1)} %bitcast.194, s32[16384]{0:T(1024)S(1)} %bitcast.195), kind=kCustom, calls=%fused_computation.1 | custom fusion | bytes 262144 | tf_op jit(solution)/shard_map/gather | solution.py:156
  (112 shorter events, 21.5 us)
Async XLA Ops:
  1.6 97.6 %collective-permute-start = (f32[4,3,128]{2,0,1:T(4,128)S(1)}, f32[4,3,128]{2,0,1:T(4,128)S(1)}, u32[]{:S(2)}, u32[]{:S(2)}) collective-permute-start(f32[4,3,128]{2,0,1:T(4,128)S(1)} %get-tuple-element.396), channel_id=1, source_target_pairs={{0,1},{1,2},{2,3},{3,4},{4,5},{5,6},{6,7},{7,8},{8,9},{9,10},{10,1... | collective-permute-start | bytes 18440 | tf_op jit(solution)/shard_map/ppermute | solution.py:22
  5.5 93.7 %collective-permute-start.1 = (f32[4,3,128]{2,0,1:T(4,128)S(1)}, f32[4,3,128]{2,0,1:T(4,128)S(1)}, u32[]{:S(2)}, u32[]{:S(2)}) collective-permute-start(f32[4,3,128]{2,0,1:T(4,128)S(1)} %get-tuple-element.397), channel_id=1, source_target_pairs={{1,0},{2,1},{3,2},{4,3},{5,4},{6,5},{7,6},{8,7},{9,8},{10,9},{11,1... | collective-permute-start | bytes 18440 | tf_op jit(solution)/shard_map/ppermute | solution.py:25
  9.3 11.1 copy-start.13
  9.3 11.4 copy-start.12
  9.3 11.6 copy-start.5
  64.9 18.1 %copy-start = (f32[512,32,32]{2,1,0:T(8,128)}, f32[512,32,32]{2,1,0:T(8,128)S(1)}, u32[]{:S(2)}) copy-start(f32[512,32,32]{2,1,0:T(8,128)S(1)} %fusion.26) | copy-start | bytes 6291460
  83.0 16.0 %copy-start.6 = (s32[128,128]{1,0:T(8,128)S(1)}, s32[128,128]{1,0:T(8,128)}, u32[]{:S(2)}) copy-start(s32[128,128]{1,0:T(8,128)} %param.20) | copy-start | bytes 196612
  83.0 16.0 %copy-start.7 = (s32[128,128]{1,0:T(8,128)S(1)}, s32[128,128]{1,0:T(8,128)}, u32[]{:S(2)}) copy-start(s32[128,128]{1,0:T(8,128)} %param.21) | copy-start | bytes 196612
  83.0 16.0 %copy-start.8 = (f32[32,512]{1,0:T(8,128)S(1)}, f32[32,512]{1,0:T(8,128)}, u32[]{:S(2)}) copy-start(f32[32,512]{1,0:T(8,128)} %param.24) | copy-start | bytes 196612
  83.0 16.2 %copy-start.1 = (f32[128,128]{1,0:T(8,128)S(1)}, f32[128,128]{1,0:T(8,128)}, u32[]{:S(2)}) copy-start(f32[128,128]{1,0:T(8,128)} %param.16) | copy-start | bytes 196612
  83.1 16.2 %copy-start.2 = (f32[128,128]{1,0:T(8,128)S(1)}, f32[128,128]{1,0:T(8,128)}, u32[]{:S(2)}) copy-start(f32[128,128]{1,0:T(8,128)} %param.17) | copy-start | bytes 196612
  83.1 16.2 %copy-start.3 = (f32[128,128]{1,0:T(8,128)S(1)}, f32[128,128]{1,0:T(8,128)}, u32[]{:S(2)}) copy-start(f32[128,128]{1,0:T(8,128)} %param.15) | copy-start | bytes 196612
  83.1 16.2 %copy-start.11 = (s32[128,4]{0,1:T(4,128)S(1)}, s32[128,4]{0,1:T(4,128)}, u32[]{:S(2)}) copy-start(s32[128,4]{0,1:T(4,128)} %param.18) | copy-start | bytes 6148
  130.7 52.6 %copy-start.4 = (f32[128,128]{1,0:T(8,128)}, f32[128,128]{1,0:T(8,128)S(1)}, u32[]{:S(2)}) copy-start(f32[128,128]{1,0:T(8,128)S(1)} %get-tuple-element.404) | copy-start | bytes 196612
  193.1 26.6 %all-to-all-start = ((f32[128,3,256]{2,1,0:T(4,128)}), f32[128,3,256]{2,1,0:T(4,128)S(1)}, u32[]{:S(2)}, u32[]{:S(2)}) async-start(f32[128,3,256]{2,1,0:T(4,128)} %bitcast.19), calls=%async_computation | async-start | bytes 1048576 | tf_op jit(solution)/shard_map/all_to_all | solution.py:64
  203.1 425.6 %copy-start.9 = (f32[32,512]{1,0:T(8,128)S(1)}, f32[32,512]{1,0:T(8,128)}, u32[]{:S(2)}) copy-start(f32[32,512]{1,0:T(8,128)} %param.23) | copy-start | bytes 196612
  628.8 20.5 %copy-start.10 = (f32[32,512]{1,0:T(8,128)S(1)}, f32[32,512]{1,0:T(8,128)}, u32[]{:S(2)}) copy-start(f32[32,512]{1,0:T(8,128)} %param.22) | copy-start | bytes 196612
  976.6 39.7 %all-to-all-start.1 = ((f32[128,1,256]{2,1,0:T(1,128)}), f32[128,1,256]{2,1,0:T(1,128)S(1)}, u32[]{:S(2)}, u32[]{:S(2)}) async-start(f32[128,1,256]{2,1,0:T(1,128)} %bitcast.37), calls=%async_computation.1 | async-start | bytes 262144 | tf_op jit(solution)/shard_map/all_to_all | solution.py:68
where the time goes:
time: 1220 us
  local copies, waits for them, and re-layouts  587 us (48%)
  other arithmetic  452 us (37%)
  matrix products  117 us (10%)
  starting transfers between devices  47.2 us (4%)
    gather x1, local copies, waits for them, and re-layouts, body(): picked = node_sens[slot_flat]  320 us
    scatter-add x1, other arithmetic, body(): jax.ops.segment_sum(inbox[:, 1, :].reshape(-1), slot_flat, slot_total)  204 us
    scatter-add x1, other arithmetic, body(): jax.ops.segment_sum(inbox[:, 0, :].reshape(-1), slot_flat, slot_total)  204 us
    gather x1, local copies, waits for them, and re-layouts, body(): seg_sens = returned_rows[owner_flat, rank_flat]  200 us
    dot_general x8, matrix products, matmul_batch(): jnp.einsum('ijn,jkn->ikn', left, right, precision=lax.Precision.HIGHEST)  115 us
    unnamed x37, local copies, waits for them, and re-layouts  58 us
    all_to_all x1, starting transfers between devices, give_back(): lax.all_to_all(reply, ('tile', 'net'), split_axis=0, concat_axis=0, tiled...  29.6 us
    reduce_sum x2, other arithmetic, couple(): jnp.sum(common_len * jnp.exp(-jnp.abs(track_i - track_j)), axis=2)  26.9 us
  transfers between devices with their start and end apart: 4, of which 1 were waited for; matrix products, arithmetic and copies ran while one was open for 9% of the time, Pallas kernels for 0%

commit v1 on v0

v1 whole, which is shorter than its diff:
```python
import jax
import jax.numpy as jnp
from jax import lax
from jax.experimental import pallas as pl
from jax.experimental.pallas import tpu as pltpu
from jax.sharding import PartitionSpec as P

RIM = 4
GROUND = 0.2
COUPLE = 0.005
SHEET = 0.02
AXES = ("tile", "net")
BF = jnp.bfloat16
F32 = jnp.float32

ROWS = 128
SEG = 128
CAPS = 256
NODES = 32
HALF = 256
VMEM_LIMIT = 48 * 1024 * 1024

NT = (((1,), (1,)), ((), ()))
NN = (((1,), (0,)), ((), ()))


def mm(left, right, dims):
    return lax.dot_general(left, right, dims, preferred_element_type=F32)


def iota_bf(rows, cols):
    return lax.broadcasted_iota(jnp.int32, (rows, cols), 0).astype(F32).astype(BF)


def spread(row, rows):
    sixteen = jnp.broadcast_to(row, (16, row.shape[1])).astype(BF)
    return jnp.concatenate([sixteen] * (rows // 16), axis=0)


def split(value):
    high = value.astype(BF).astype(F32)
    return high, (value - high).astype(BF).astype(F32)


def rank_kernel(owner_ref, rank_ref):
    iota = lax.broadcasted_iota(jnp.int32, (ROWS, SEG), 0)
    r0 = lax.broadcasted_iota(jnp.int32, (SEG, 2 * SEG), 0)
    c0 = lax.broadcasted_iota(jnp.int32, (SEG, 2 * SEG), 1)
    upper = jnp.where((r0 <= c0), 1.0, 0.0).astype(BF)

    def step(g, before):
        for j in range(8):
            b = g * 8 + j
            hit = iota == owner_ref[pl.ds(b, 1), :]
            ones = jnp.where(hit, 1.0, 0.0).astype(BF)
            sums = mm(ones, upper, NN)
            placed = jnp.where(hit, sums[:, :SEG] + before, 0.0)
            rank_ref[pl.ds(b, 1), :] = jnp.sum(placed, axis=0, keepdims=True) - 1.0
            before = before + sums[:, SEG:]
        return before

    lax.fori_loop(0, ROWS // 8, step, jnp.zeros((ROWS, SEG), F32))


def couple_kernel(first_ref, nbr_ref, start_ref, len_ref, track_ref, low_ref, high_ref, out_ref,
                  s_j, e_j, g_j, f_j, s_t, e_t, g_t, res_t):
    def fill(at, count, start, length, track):
        s_j[pl.ds(at, count), :] = start
        e_j[pl.ds(at, count), :] = start + length
        g_j[pl.ds(at, count), :] = jnp.exp(2.0 * track)
        f_j[pl.ds(at, count), :] = jnp.exp(-track)

    start, length, track = start_ref[...], len_ref[...], track_ref[...]
    fill(8, ROWS, start, length, track)
    fill(0, 8, low_ref[0:8, :], low_ref[8:16, :], low_ref[16:24, :])
    fill(8 + ROWS, 8, high_ref[0:8, :], high_ref[8:16, :], high_ref[16:24, :])
    s_t[...] = start.T
    e_t[...] = (start + length).T
    g_t[...] = jnp.exp(2.0 * track).T
    lane = lax.broadcasted_iota(jnp.int32, (8, SEG), 1)
    first = first_ref[0]

    def step(b, carry):
        column = jnp.full((8, SEG), b, jnp.int32)
        rows = []
        for k in range(4):
            near = jnp.clip(nbr_ref[b, k] - first + 8, 0, ROWS + 15)
            rows.append([
                jnp.broadcast_to(ref[pl.ds(near, 1), :], (8, SEG)) for ref in (s_j, e_j, g_j, f_j)
            ])
        for t in range(SEG // 8):
            part = slice(8 * t, 8 * t + 8)
            si = jnp.take_along_axis(s_t[part, :], column, axis=1)
            ei = jnp.take_along_axis(e_t[part, :], column, axis=1)
            gi = jnp.take_along_axis(g_t[part, :], column, axis=1)
            total = None
            for sj, ej, gj, fj in rows:
                common = jnp.maximum(jnp.minimum(ei, ej) - jnp.maximum(si, sj), 0.0)
                term = common * (jnp.minimum(gi, gj) * fj)
                total = term if total is None else total + term
            summed = jnp.sum(total, axis=1, keepdims=True)
            res_t[part, :] = jnp.where(lane == b, summed, res_t[part, :])
        return carry

    lax.fori_loop(0, ROWS, step, 0)
    out_ref[...] = GROUND * length + COUPLE * f_j[8:8 + ROWS, :] * res_t[...].T


def outbox_kernel(owner_ref, rank_ref, cap_ref, len_ref, local_ref, node_ref, out_ref,
                  own, pieces, left, right, acc):
    own[...] = owner_ref[...].astype(F32)
    local, node = local_ref[...], node_ref[...]
    cap_hi, cap_lo = split(cap_ref[...])
    res_hi, res_lo = split(SHEET * len_ref[...])
    upper = (local >> 8) * NODES + node
    values = [cap_hi, cap_lo, res_hi, res_lo,
              (upper * HALF).astype(F32), (local & (HALF - 1)).astype(F32)]
    for p, value in enumerate(values):
        pieces[p * ROWS:(p + 1) * ROWS, :] = value
    acc[...] = jnp.zeros_like(acc)
    iota_o = iota_bf(ROWS, SEG)
    iota_r = iota_bf(CAPS, SEG)
    zero, one = jnp.zeros((), BF), jnp.ones((), BF)

    def step(g, carry):
        for j in range(8):
            b = g * 8 + j
            lanes = slice(j * SEG, (j + 1) * SEG)
            hit = iota_o == spread(own[pl.ds(b, 1), :], ROWS)
            for p in range(6):
                value = spread(pieces[pl.ds(p * ROWS + b, 1), :], ROWS)
                left[p * ROWS:(p + 1) * ROWS, lanes] = jnp.where(hit, value, zero)
            right[:, lanes] = jnp.where(iota_r == spread(rank_ref[pl.ds(b, 1), :], CAPS), one, zero)
        acc[...] += mm(left[...], right[...], NT)
        return carry

    lax.fori_loop(0, ROWS // 8, step, 0)
    for v in range(3):
        high = acc[2 * v * ROWS:(2 * v + 1) * ROWS, :]
        low = acc[(2 * v + 1) * ROWS:(2 * v + 2) * ROWS, :]
        out_ref[:, v * CAPS:(v + 1) * CAPS] = high + low


def owner_kernel(inbox_ref, pin_ref, load_ref, weight_ref, parent_ref, delay_ref, reply_ref,
                 upper_s, lower_s, pieces, left, right, acc):
    slot = inbox_ref[:, 2 * CAPS:].astype(jnp.int32)
    upper_s[...] = (slot >> 8).astype(F32)
    lower_s[...] = (slot & (HALF - 1)).astype(F32)
    for v in range(2):
        high, low = split(inbox_ref[:, v * CAPS:(v + 1) * CAPS])
        pieces[2 * v * ROWS:(2 * v + 1) * ROWS, :] = high
        pieces[(2 * v + 1) * ROWS:(2 * v + 2) * ROWS, :] = low
    acc[...] = jnp.zeros_like(acc)
    iota_u = iota_bf(64, CAPS)
    iota_l = iota_bf(HALF, CAPS)
    zero, one = jnp.zeros((), BF), jnp.ones((), BF)

    def collect(g, carry):
        for j in range(4):
            s = g * 4 + j
            lanes = slice(j * CAPS, (j + 1) * CAPS)
            hit = iota_u == spread(upper_s[pl.ds(s, 1), :], 64)
            for p in range(4):
                value = spread(pieces[pl.ds(p * ROWS + s, 1), :], 64)
                left[p * 64:(p + 1) * 64, lanes] = jnp.where(hit, value, zero)
            right[:, lanes] = jnp.where(iota_l == spread(lower_s[pl.ds(s, 1), :], HALF), one, zero)
        acc[...] += mm(left[...], right[...], NT)
        return carry

    lax.fori_loop(0, ROWS // 4, collect, 0)

    def table(at):
        both = acc[at:at + 64, :] + acc[at + 64:at + 128, :]
        return jnp.concatenate([both[:NODES], both[NODES:]], axis=1)

    cap = load_ref[...] + table(0)
    res = pin_ref[...] + table(128)
    weight = weight_ref[...]
    iota8 = lax.broadcasted_iota(jnp.int32, (8, 2 * HALF), 0)
    tiles = NODES // 8
    cut = lambda a: [a[8 * t:8 * t + 8, :] for t in range(tiles)]
    sub, below, res = cut(cap), cut(weight), cut(res)
    for k in range(NODES - 1, 0, -1):
        t, r = divmod(k, 8)
        parent = jnp.broadcast_to(parent_ref[k:k + 1, :], iota8.shape)
        sub_k = jnp.broadcast_to(sub[t][r:r + 1, :], iota8.shape)
        below_k = jnp.broadcast_to(below[t][r:r + 1, :], iota8.shape)
        for a in range((k - 1) // 8 + 1):
            hit = parent == iota8 + 8 * a
            sub[a] = sub[a] + jnp.where(hit, sub_k, 0.0)
            below[a] = below[a] + jnp.where(hit, below_k, 0.0)
    step_d = [res[t] * sub[t] for t in range(tiles)]
    step_g = [res[t] * below[t] for t in range(tiles)]
    down_d, down_g = list(step_d), list(step_g)
    for k in range(1, NODES):
        t, r = divmod(k, 8)
        parent = jnp.broadcast_to(parent_ref[k:k + 1, :], iota8.shape)
        from_d = from_g = None
        for a in range((k - 1) // 8 + 1):
            hit = parent == iota8 + 8 * a
            d, g = jnp.where(hit, down_d[a], 0.0), jnp.where(hit, down_g[a], 0.0)
            from_d = d if from_d is None else from_d + d
            from_g = g if from_g is None else from_g + g
        here = iota8 == r
        down_d[t] = jnp.where(here, step_d[t] + jnp.sum(from_d, axis=0, keepdims=True), down_d[t])
        down_g[t] = jnp.where(here, step_g[t] + jnp.sum(from_g, axis=0, keepdims=True), down_g[t])
    delay_ref[...] = jnp.concatenate(down_d, axis=0)
    sens = jnp.concatenate(
        [SHEET * (below[t] * sub[t]) + GROUND * down_g[t] for t in range(tiles)], axis=0)
    high, low = split(sens)
    picks = jnp.concatenate(
        [high[:, :HALF], high[:, HALF:], low[:, :HALF], low[:, HALF:]], axis=0).astype(BF)
    iota_uf = lax.broadcasted_iota(jnp.int32, (64, CAPS), 0).astype(F32)

    def answer(g, carry):
        for j in range(4):
            s = g * 4 + j
            ones = jnp.where(iota_l == spread(lower_s[pl.ds(s, 1), :], HALF), one, zero)
            found = mm(picks, ones, NN)
            kept = jnp.where(iota_uf == upper_s[pl.ds(s, 1), :], found[:64] + found[64:], 0.0)
            reply_ref[pl.ds(s, 1), :] = jnp.sum(kept, axis=0, keepdims=True)
        return carry

    lax.fori_loop(0, ROWS // 4, answer, 0)


def final_kernel(returned_ref, owner_ref, rank_ref, out_ref):
    high, low = split(returned_ref[...])
    picks = jnp.concatenate([high, low], axis=0).astype(BF)
    iota_r = iota_bf(CAPS, 2 * SEG)
    iota_o = lax.broadcasted_iota(jnp.int32, (ROWS, 2 * SEG), 0)
    zero, one = jnp.zeros((), BF), jnp.ones((), BF)

    def pair(ref, b):
        return jnp.concatenate([ref[pl.ds(b, 1), :], ref[pl.ds(b + 1, 1), :]], axis=1)

    def step(g, carry):
        for j in range(0, 8, 2):
            b = g * 8 + j
            ones = jnp.where(iota_r == spread(pair(rank_ref, b), CAPS), one, zero)
            found = mm(picks, ones, NN)
            kept = jnp.where(iota_o == pair(owner_ref, b), found[:ROWS] + found[ROWS:], 0.0)
            row = jnp.sum(kept, axis=0, keepdims=True)
            out_ref[pl.ds(b, 1), :] = row[:, :SEG]
            out_ref[pl.ds(b + 1, 1), :] = row[:, SEG:]
        return carry

    lax.fori_loop(0, ROWS // 8, step, 0)


def call(kernel, name, shapes, in_specs, scratch=()):
    vmem = pl.BlockSpec(memory_space=pltpu.VMEM)
    smem = pl.BlockSpec(memory_space=pltpu.SMEM)
    specs = [smem if c == "s" else vmem for c in in_specs]
    outs = [jax.ShapeDtypeStruct(shape, F32) for shape in shapes]
    single = len(outs) == 1
    return pl.pallas_call(
        kernel,
        out_shape=outs[0] if single else outs,
        in_specs=specs,
        out_specs=vmem if single else [vmem] * len(outs),
        scratch_shapes=[pltpu.VMEM(shape, dtype) for shape, dtype in scratch],
        compiler_params=pltpu.CompilerParams(vmem_limit_bytes=VMEM_LIMIT),
        name=name,
    )


def exchange(box):
    return lax.all_to_all(box, AXES, split_axis=0, concat_axis=0, tiled=True)


def body(seg_start, seg_len, seg_track, seg_nbr, seg_owner, seg_local, seg_node,
         pin_res, load_cap, crit_weight, net_parent):
    devices = lax.axis_size(AXES)
    forward = [(i, i + 1) for i in range(devices - 1)]
    backward = [(i + 1, i) for i in range(devices - 1)]
    feats = (seg_start, seg_len, seg_track)
    low = lax.ppermute(jnp.concatenate([f[-8:] for f in feats], axis=0), AXES, forward)
    high = lax.ppermute(jnp.concatenate([f[:8] for f in feats], axis=0), AXES, backward)
    owner = seg_owner.reshape(ROWS, SEG)
    square, flat = (ROWS, SEG), (ROWS, CAPS)
    rank = call(rank_kernel, "rank", [square], "v")(owner)
    first = (lax.axis_index(AXES) * ROWS).astype(jnp.int32).reshape(1)
    wide = (ROWS + 16, SEG)
    seg_cap = call(
        couple_kernel, "couple", [square], "ssvvvvv",
        [(wide, F32)] * 4 + [(square, F32)] * 4,
    )(first, seg_nbr, seg_start, seg_len, seg_track, low, high)
    outbox = call(
        outbox_kernel, "outbox", [(ROWS, 3 * CAPS)], "vvvvvv",
        [(square, F32), ((6 * ROWS, SEG), F32), ((6 * ROWS, 8 * SEG), BF), ((CAPS, 8 * SEG), BF),
         ((6 * ROWS, CAPS), F32)],
    )(owner, rank, seg_cap, seg_len, seg_local, seg_node)
    inbox = exchange(outbox)
    delay, reply = call(
        owner_kernel, "owner", [(NODES, 2 * HALF), flat], "vvvvv",
        [(flat, F32), (flat, F32), ((4 * ROWS, CAPS), F32), ((CAPS, 4 * CAPS), BF),
         ((HALF, 4 * CAPS), BF), ((CAPS, HALF), F32)],
    )(inbox, pin_res, load_cap, crit_weight, net_parent)
    returned = exchange(reply)
    seg_sens = call(final_kernel, "final", [square], "vvv")(returned, owner, rank)
    return seg_cap, delay, seg_sens


def solution(mesh):
    rows, nets = P(AXES, None), P(None, AXES)
    placed = (rows, rows, rows, rows, P(AXES, None, None), rows, rows, nets, nets, nets, nets)
    return jax.shard_map(body, mesh=mesh, in_specs=placed, out_specs=(rows, nets, rows), check_vma=False)
```

time: 1220 us -> 171 us (0.14)
  local copies, waits for them, and re-layouts: 587 us -> 4.61 us
  other arithmetic: 452 us -> 0.01 us
  Pallas kernels: 0 us -> 122 us
  matrix products: 117 us -> 0 us
  starting transfers between devices: 47.2 us -> 7.69 us
  blocking collectives: 0 us -> 36.1 us
    gather x2 -> x0, local copies, waits for them, and re-layouts: 520 us -> none  [the longest x1 320 us: body(): picked = node_sens[slot_flat]]
    scatter-add x2 -> x0, other arithmetic: 408 us -> none  [the longest x1 204 us: body(): jax.ops.segment_sum(inbox[:, 1, :].reshape(-1), slot_flat, slot_total)]
    pallas_call x0 -> x5, Pallas kernels: none -> 122 us  [the longest x1 80.1 us: body(): call(couple_kernel, 'couple', [square], 'ssvvvvv', [(wide, F32)] * 4 + [(...]
    dot_general x10 -> x0, matrix products: 117 us -> none  [the longest x8 115 us: matmul_batch(): jnp.einsum('ijn,jkn->ikn', left, right, precision=lax.Precision.HIGHEST)]
    unnamed x37 -> x27, local copies, waits for them, and re-layouts: 58 us -> 2.59 us
    all_to_all x2 -> x0, starting transfers between devices: 39.5 us -> none  [the longest x1 29.6 us: give_back(): lax.all_to_all(reply, ('tile', 'net'), split_axis=0, concat_axis=0, tiled...]
    all_to_all x0 -> x2, blocking collectives: none -> 36.1 us  [exchange(): return lax.all_to_all(box, AXES, split_axis=0, concat_axis=0, tiled=True)]
    reduce_sum x6 -> x0, other arithmetic: 32.2 us -> none  [the longest x2 26.9 us: couple(): jnp.sum(common_len * jnp.exp(-jnp.abs(track_i - track_j)), axis=2)]
  transfers between devices with their start and end apart: 4 -> 2, of which waited for: 1 -> 0; matrix products, arithmetic and copies ran while one was open for 9% -> 0% of each run, Pallas kernels for 0% -> 3%
where the time goes in v1:
time: 171 us
  Pallas kernels  122 us (71%)
  blocking collectives  36.1 us (21%)
  starting transfers between devices  7.69 us (4%)
  local copies, waits for them, and re-layouts  4.61 us (3%)
    pallas_call x1, Pallas kernels, body(): call(couple_kernel, 'couple', [square], 'ssvvvvv', [(wide, F32)] * 4 + [(...  80.1 us
    all_to_all x2, blocking collectives, exchange(): return lax.all_to_all(box, AXES, split_axis=0, concat_axis=0, tiled=True)  36.1 us
    pallas_call x1, Pallas kernels, body(): call(owner_kernel, 'owner', [(NODES, 2 * HALF), flat], 'vvvvv', [(flat, F...  20.4 us
    pallas_call x1, Pallas kernels, body(): call(outbox_kernel, 'outbox', [(ROWS, 3 * CAPS)], 'vvvvvv', [(square, F32...  10.8 us
    pallas_call x1, Pallas kernels, body(): call(final_kernel, 'final', [square], 'vvv')(returned, owner, rank)  5.76 us
    pallas_call x1, Pallas kernels, body(): rank = call(rank_kernel, 'rank', [square], 'v')(owner)  4.79 us
    ppermute x1, starting transfers between devices, body(): lax.ppermute(jnp.concatenate([f[-8:] for f in feats], axis=0), AXES, forw...  3.94 us
    ppermute x1, starting transfers between devices, body(): lax.ppermute(jnp.concatenate([f[:8] for f in feats], axis=0), AXES, backw...  3.75 us
  transfers between devices with their start and end apart: 2, of which 0 were waited for; matrix products, arithmetic and copies ran while one was open for 0% of the time, Pallas kernels for 3%

profile of v1, /device:TPU:1, one launch (start us, length us, event | category | flops | bytes accessed | tf_op | source)
XLA Modules:
  0.0 171.1 jit_solution(4201498739896662904)
XLA Ops:
  0.6 0.7 fusion.2
  1.4 0.7 fusion
  2.1 3.9 %collective-permute-start = (f32[24,128]{1,0:T(8,128)S(1)}, f32[24,128]{1,0:T(8,128)S(1)}, u32[]{:S(2)}, u32[]{:S(2)}) collective-permute-start(f32[24,128]{1,0:T(8,128)S(1)} %pad_maximum_fusion), channel_id=1, source_target_pairs={{0,1},{1,2},{2,3},{3,4},{4,5},{5,6},{6,7},{7,8},{8,9},{9,10},{10,1... | collective-permute-start | bytes 36872 | tf_op jit(solution)/shard_map/ppermute | solution.py:278
  6.1 3.7 %collective-permute-start.1 = (f32[24,128]{1,0:T(8,128)S(1)}, f32[24,128]{1,0:T(8,128)S(1)}, u32[]{:S(2)}, u32[]{:S(2)}) collective-permute-start(f32[24,128]{1,0:T(8,128)S(1)} %pad_maximum_fusion.1), channel_id=1, source_target_pairs={{1,0},{2,1},{3,2},{4,3},{5,4},{6,5},{7,6},{8,7},{9,8},{10,9},{11,1... | collective-permute-start | bytes 36872 | tf_op jit(solution)/shard_map/ppermute | solution.py:279
  9.8 0.0 copy-start.11
  9.9 0.0 copy-start.3
  9.9 0.0 copy-start.4
  9.9 4.8 %rank.1.rank_ref = f32[128,128]{1,0:T(8,128)S(1)} custom-call(s32[128,128]{1,0:T(8,128)S(1)} %bitcast.12), custom_call_target="tpu_custom_call" | custom-call | tf_op jit(solution)/shard_map/rank/pallas_call | solution.py:282
  14.7 0.0 copy-start.1
  14.7 0.1 copy.15.nbr_ref
  14.9 0.7 copy-done.1
  15.5 80.1 %couple.1.cap_ref = f32[128,128]{1,0:T(8,128)} custom-call(s32[1]{0:T(128)} %bitcast.first_ref, s32[128,4]{1,0:T(8,128)S(1)} %copy.15.nbr_ref, f32[128,128]{1,0:T(8,128)S(1)} %copy-done.4, f32[128,128]{1,0:T(8,128)S(1)} %copy-done.1, f32[128,128]{1,0:T(8,128)S(1)} %copy-done.3, f32[24,128]{1,0:T(8,128)S(1)} %collective-permute-done.low_ref, ...), custom_call_target="tpu_custom_call" | custom-call | tf_op jit(solution)/shard_map/couple/pallas_call | solution.py:285
  95.7 0.8 copy-done.2
  96.5 10.8 %outbox.1 = f32[128,768]{1,0:T(8,128)S(1)} custom-call(s32[128,128]{1,0:T(8,128)S(1)} %bitcast.13, f32[128,128]{1,0:T(8,128)S(1)} %rank.1.rank_ref, f32[128,128]{1,0:T(8,128)S(1)} %copy-done.2, f32[128,128]{1,0:T(8,128)S(1)} %copy-done.1, s32[128,128]{1,0:T(8,128)S(1)} %copy-done.5, s32[128,128]{1,0:T(8,128)S(1)} %copy-done.6), custom_call_target="tpu_custom_call" | custom-call | tf_op jit(solution)/shard_map/outbox/pallas_call | solution.py:289
  107.3 0.4 copy.16
  107.8 22.2 %all_to_all.22 = f32[128,1,768]{2,1,0:T(1,128)S(1)} all-to-all(f32[128,1,768]{2,1,0:T(1,128)S(1)} %copy.16), channel_id=1, replica_groups=mesh['tile'=32,'net'=4] {'tile','net'}, dimensions={0} | all-to-all | bytes 786432 | tf_op jit(solution)/shard_map/all_to_all | solution.py:269
  130.0 0.8 copy-done.7
  130.8 0.0 copy-done.8
  130.8 0.0 copy-done.9
  130.8 0.0 copy-done.10
  130.9 20.4 %owner.1 = (f32[32,512]{1,0:T(8,128)}, f32[128,256]{1,0:T(8,128)S(1)}) custom-call(f32[128,768]{1,0:T(8,128)S(1)} %bitcast.10, f32[32,512]{1,0:T(8,128)S(1)} %copy-done.7, f32[32,512]{1,0:T(8,128)S(1)} %copy-done.8, f32[32,512]{1,0:T(8,128)S(1)} %copy-done.9, s32[32,512]{1,0:T(8,128)S(1)} %copy-done.10), custom_call_target="tpu_custom_call" | custom-call | tf_op jit(solution)/shard_map/owner/pallas_call | solution.py:295
  151.3 0.1 copy.17
  151.4 13.9 %all_to_all.23 = f32[128,1,256]{2,1,0:T(1,128)S(1)} all-to-all(f32[128,1,256]{2,1,0:T(1,128)S(1)} %copy.17), channel_id=1, replica_groups=mesh['tile'=32,'net'=4] {'tile','net'}, dimensions={0} | all-to-all | bytes 262144 | tf_op jit(solution)/shard_map/all_to_all | solution.py:269
  165.3 5.8 %final.1 = f32[128,128]{1,0:T(8,128)} custom-call(f32[128,256]{1,0:T(8,128)S(1)} %bitcast.15, s32[128,128]{1,0:T(8,128)S(1)} %bitcast.14, f32[128,128]{1,0:T(8,128)S(1)} %rank.1.rank_ref), custom_call_target="tpu_custom_call" | custom-call | tf_op jit(solution)/shard_map/final/pallas_call | solution.py:301
  (20 shorter events, 0.1 us)
Async XLA Ops:
  0.6 9.2 %copy-start = (s32[128,128,1]{1,2,0:T(1,128)S(1)}, s32[128,128,1]{1,2,0:T(1,128)}, u32[]{:S(2)}) copy-start(s32[128,128,1]{1,2,0:T(1,128)} %param.15) | copy-start | bytes 196612
  2.1 12.7 %collective-permute-start = (f32[24,128]{1,0:T(8,128)S(1)}, f32[24,128]{1,0:T(8,128)S(1)}, u32[]{:S(2)}, u32[]{:S(2)}) collective-permute-start(f32[24,128]{1,0:T(8,128)S(1)} %pad_maximum_fusion), channel_id=1, source_target_pairs={{0,1},{1,2},{2,3},{3,4},{4,5},{5,6},{6,7},{7,8},{8,9},{9,10},{10,1... | collective-permute-start | bytes 36872 | tf_op jit(solution)/shard_map/ppermute | solution.py:278
  6.1 8.8 %collective-permute-start.1 = (f32[24,128]{1,0:T(8,128)S(1)}, f32[24,128]{1,0:T(8,128)S(1)}, u32[]{:S(2)}, u32[]{:S(2)}) collective-permute-start(f32[24,128]{1,0:T(8,128)S(1)} %pad_maximum_fusion.1), channel_id=1, source_target_pairs={{1,0},{2,1},{3,2},{4,3},{5,4},{6,5},{7,6},{8,7},{9,8},{10,9},{11,1... | collective-permute-start | bytes 36872 | tf_op jit(solution)/shard_map/ppermute | solution.py:279
  9.8 4.8 %copy-start.11 = (s32[128,4]{0,1:T(4,128)S(1)}, s32[128,4]{0,1:T(4,128)}, u32[]{:S(2)}) copy-start(s32[128,4]{0,1:T(4,128)} %param.14) | copy-start | bytes 6148
  9.9 5.0 %copy-start.3 = (f32[128,128]{1,0:T(8,128)S(1)}, f32[128,128]{1,0:T(8,128)}, u32[]{:S(2)}) copy-start(f32[128,128]{1,0:T(8,128)} %track_ref.1) | copy-start | bytes 196612
  9.9 5.0 %copy-start.4 = (f32[128,128]{1,0:T(8,128)S(1)}, f32[128,128]{1,0:T(8,128)}, u32[]{:S(2)}) copy-start(f32[128,128]{1,0:T(8,128)} %start_ref.1) | copy-start | bytes 196612
  14.7 0.8 copy-start.1
  15.5 80.2 %copy-start.5 = (s32[128,128]{1,0:T(8,128)S(1)}, s32[128,128]{1,0:T(8,128)}, u32[]{:S(2)}) copy-start(s32[128,128]{1,0:T(8,128)} %local_ref.1) | copy-start | bytes 196612
  15.5 80.2 %copy-start.6 = (s32[128,128]{1,0:T(8,128)S(1)}, s32[128,128]{1,0:T(8,128)}, u32[]{:S(2)}) copy-start(s32[128,128]{1,0:T(8,128)} %node_ref.1) | copy-start | bytes 196612
  95.7 0.8 copy-start.2
  129.9 0.8 copy-start.7
  129.9 0.9 copy-start.8
  129.9 0.9 copy-start.9
  129.9 0.9 copy-start.10

commit v2 on v1

v2 whole, which is shorter than its diff:
```python
import jax
import jax.numpy as jnp
from jax import lax
from jax.experimental import pallas as pl
from jax.experimental.pallas import tpu as pltpu
from jax.sharding import PartitionSpec as P

RIM = 4
GROUND = 0.2
COUPLE = 0.005
SHEET = 0.02
AXES = ("tile", "net")
BF = jnp.bfloat16
F32 = jnp.float32

ROWS = 128
SEG = 128
CAPS = 256
NODES = 32
HALF = 256
VMEM_LIMIT = 48 * 1024 * 1024

NT = (((1,), (1,)), ((), ()))
NN = (((1,), (0,)), ((), ()))


def mm(left, right, dims):
    return lax.dot_general(left, right, dims, preferred_element_type=F32)


def iota_bf(rows, cols):
    return lax.broadcasted_iota(jnp.int32, (rows, cols), 0).astype(F32).astype(BF)


def spread(row, rows):
    sixteen = jnp.broadcast_to(row, (16, row.shape[1])).astype(BF)
    return jnp.concatenate([sixteen] * (rows // 16), axis=0)


def split(value):
    high = value.astype(BF).astype(F32)
    return high, (value - high).astype(BF).astype(F32)


def rank_kernel(owner_ref, rank_ref):
    iota = lax.broadcasted_iota(jnp.int32, (ROWS, SEG), 0)
    r0 = lax.broadcasted_iota(jnp.int32, (SEG, 2 * SEG), 0)
    c0 = lax.broadcasted_iota(jnp.int32, (SEG, 2 * SEG), 1)
    upper = jnp.where((r0 <= c0), 1.0, 0.0).astype(BF)

    def step(g, before):
        for j in range(8):
            b = g * 8 + j
            hit = iota == owner_ref[pl.ds(b, 1), :]
            ones = jnp.where(hit, 1.0, 0.0).astype(BF)
            sums = mm(ones, upper, NN)
            placed = jnp.where(hit, sums[:, :SEG] + before, 0.0)
            rank_ref[pl.ds(b, 1), :] = jnp.sum(placed, axis=0, keepdims=True) - 1.0
            before = before + sums[:, SEG:]
        return before

    lax.fori_loop(0, ROWS // 8, step, jnp.zeros((ROWS, SEG), F32))


def split3(value):
    high = value.astype(BF).astype(F32)
    rest = value - high
    middle = rest.astype(BF).astype(F32)
    return [high, middle, rest - middle]


def eight(ref, group):
    return ref[pl.ds(pl.multiple_of(group * 8, 8), 8), :]


def couple_kernel(first_ref, nbr_ref, start_ref, len_ref, track_ref, low_ref, high_ref,
                  owner_ref, rank_ref, local_ref, node_ref, cap_ref, out_ref,
                  s_j, e_j, g_j, f_j, pick, shown, full_a, full_b,
                  left_a, left_b, right_a, right_b, acc):
    def fill(at, count, start, length, track):
        s_j[at:at + count, :] = start
        e_j[at:at + count, :] = start + length
        g_j[at:at + count, :] = jnp.exp(2.0 * track)
        f_j[at:at + count, :] = jnp.exp(-track)

    fill(8, ROWS, start_ref[...], len_ref[...], track_ref[...])
    fill(0, 8, low_ref[0:8, :], low_ref[8:16, :], low_ref[16:24, :])
    fill(8 + ROWS, 8, high_ref[0:8, :], high_ref[8:16, :], high_ref[16:24, :])
    row = lax.broadcasted_iota(jnp.int32, (SEG, 6 * SEG), 0)
    col = lax.broadcasted_iota(jnp.int32, (SEG, 6 * SEG), 1) >> 7
    array = jnp.where(row < 24, 0, jnp.where(row < 48, 1, jnp.where(row < 72, 2, 9)))
    pick[...] = jnp.where((row & 1) * 3 + array == col, 1.0, 0.0).astype(BF)
    pair_of = (lax.broadcasted_iota(jnp.int32, (SEG, SEG), 1) & 7) >> 1
    lane = lax.broadcasted_iota(jnp.int32, (8, SEG), 1)
    iota_o = iota_bf(ROWS, SEG)
    iota_r = iota_bf(CAPS, SEG)
    zero, one = jnp.zeros((), BF), jnp.ones((), BF)
    first = first_ref[0]

    def spread_columns(g, full):
        at = pl.ds(pl.multiple_of(8 + g * 8, 8), 8)
        pieces = split3(s_j[at, :]) + split3(e_j[at, :]) + split3(g_j[at, :])
        turned = jnp.concatenate(pieces + [jnp.zeros((SEG - 72, SEG), F32)], axis=0).T
        for pair in range(4):
            shown[pair * SEG:(pair + 1) * SEG, :] = jnp.where(pair_of == pair, turned, 0.0).astype(BF)
        full[...] = mm(shown[...], pick[...], NN)

    def pairs(g, j, full, sums):
        rows = []
        for k in range(4):
            near = jnp.clip(nbr_ref[g * 8 + j, k] - first + 8, 0, ROWS + 15)
            rows.append([
                jnp.broadcast_to(ref[pl.ds(near, 1), :], (8, SEG)) for ref in (s_j, e_j, g_j, f_j)
            ])
        base = (j & 1) * 3 * SEG
        for t in range(SEG // 8):
            part = slice((j >> 1) * SEG + 8 * t, (j >> 1) * SEG + 8 * t + 8)
            si = full[part, base:base + SEG]
            ei = full[part, base + SEG:base + 2 * SEG]
            gi = full[part, base + 2 * SEG:base + 3 * SEG]
            total = None
            for sj, ej, gj, fj in rows:
                common = jnp.maximum(jnp.minimum(ei, ej) - jnp.maximum(si, sj), 0.0)
                term = common * (jnp.minimum(gi, gj) * fj)
                total = term if total is None else total + term
            sums[t] = jnp.where(lane == j, jnp.sum(total, axis=1, keepdims=True), sums[t])

    def values_of(g):
        local, node = eight(local_ref, g), eight(node_ref, g)
        cap_hi, cap_lo = split(eight(cap_ref, g))
        res_hi, res_lo = split(SHEET * eight(len_ref, g))
        upper = (local >> 8) * NODES + node
        return [cap_hi, cap_lo, res_hi, res_lo,
                (upper * HALF).astype(F32), (local & (HALF - 1)).astype(F32)]

    def build(j, owner, rank, values, left, right):
        lanes = slice(j * SEG, (j + 1) * SEG)
        hit = iota_o == spread(owner[j:j + 1, :], ROWS)
        for p in range(6):
            value = spread(values[p][j:j + 1, :], ROWS)
            left[p * ROWS:(p + 1) * ROWS, lanes] = jnp.where(hit, value, zero)
        right[:, lanes] = jnp.where(iota_r == spread(rank[j:j + 1, :], CAPS), one, zero)

    def step(g, full, full_next, left, right, left_old, right_old):
        acc[...] += mm(left_old[...], right_old[...], NT)
        spread_columns(jnp.minimum(g + 1, ROWS // 8 - 1), full_next)
        last = jnp.maximum(g - 1, 0)
        owner = jnp.where(g > 0, eight(owner_ref, last).astype(F32), -1.0)
        rank, values = eight(rank_ref, last), values_of(last)
        sums = [jnp.zeros((8, SEG), F32)] * (SEG // 8)
        for j in range(8):
            build(j, owner, rank, values, left, right)
            pairs(g, j, full, sums)
        summed = jnp.concatenate(sums, axis=0).T[:8, :]
        at = pl.ds(pl.multiple_of(g * 8, 8), 8)
        scale = f_j[pl.ds(pl.multiple_of(8 + g * 8, 8), 8), :]
        cap_ref[at, :] = GROUND * len_ref[at, :] + COUPLE * scale * summed

    def two(h, carry):
        step(2 * h, full_a, full_b, left_a, right_a, left_b, right_b)
        step(2 * h + 1, full_b, full_a, left_b, right_b, left_a, right_a)
        return carry

    acc[...] = jnp.zeros_like(acc)
    cap_ref[0:8, :] = jnp.zeros((8, SEG), F32)
    left_b[...] = jnp.zeros_like(left_b)
    right_b[...] = jnp.zeros_like(right_b)
    spread_columns(0, full_a)
    lax.fori_loop(0, ROWS // 16, two, 0)
    last = ROWS // 8 - 1
    owner, rank, values = eight(owner_ref, last).astype(F32), eight(rank_ref, last), values_of(last)
    for j in range(8):
        build(j, owner, rank, values, left_a, right_a)
    acc[...] += mm(left_b[...], right_b[...], NT)
    acc[...] += mm(left_a[...], right_a[...], NT)
    for v in range(3):
        high = acc[2 * v * ROWS:(2 * v + 1) * ROWS, :]
        low = acc[(2 * v + 1) * ROWS:(2 * v + 2) * ROWS, :]
        out_ref[:, v * CAPS:(v + 1) * CAPS] = high + low


def owner_kernel(inbox_ref, pin_ref, load_ref, weight_ref, parent_ref, delay_ref, reply_ref,
                 upper_s, lower_s, pieces, left_a, left_b, right_a, right_b, found_a, found_b, acc):
    slot = inbox_ref[:, 2 * CAPS:].astype(jnp.int32)
    upper_s[...] = (slot >> 8).astype(F32)
    lower_s[...] = (slot & (HALF - 1)).astype(F32)
    for v in range(2):
        high, low = split(inbox_ref[:, v * CAPS:(v + 1) * CAPS])
        pieces[2 * v * ROWS:(2 * v + 1) * ROWS, :] = high
        pieces[(2 * v + 1) * ROWS:(2 * v + 2) * ROWS, :] = low
    acc[...] = jnp.zeros_like(acc)
    iota_u = iota_bf(64, CAPS)
    iota_l = iota_bf(HALF, CAPS)
    zero, one = jnp.zeros((), BF), jnp.ones((), BF)
    units = ROWS // 8

    def build_right(u, right):
        lower = eight(lower_s, u)
        for j in range(8):
            right[:, j * CAPS:(j + 1) * CAPS] = jnp.where(
                iota_l == spread(lower[j:j + 1, :], HALF), one, zero)

    def build_left(u, left):
        upper = eight(upper_s, u)
        values = [pieces[pl.ds(pl.multiple_of(p * ROWS + u * 8, 8), 8), :] for p in range(4)]
        for j in range(8):
            hit = iota_u == spread(upper[j:j + 1, :], 64)
            for p in range(4):
                left[p * 64:(p + 1) * 64, j * CAPS:(j + 1) * CAPS] = jnp.where(
                    hit, spread(values[p][j:j + 1, :], 64), zero)

    def collect(h, carry):
        for u, now, later in (
            (2 * h + 1, (left_a, right_a), (left_b, right_b)),
            (jnp.minimum(2 * h + 2, units - 1), (left_b, right_b), (left_a, right_a)),
        ):
            acc[...] += mm(now[0][...], now[1][...], NT)
            build_left(u, later[0])
            build_right(u, later[1])
        return carry

    build_left(0, left_a)
    build_right(0, right_a)
    lax.fori_loop(0, units // 2, collect, 0)

    def table(at):
        both = acc[at:at + 64, :] + acc[at + 64:at + 128, :]
        return jnp.concatenate([both[:NODES], both[NODES:]], axis=1)

    build_right(0, right_a)
    build_right(1, right_b)
    cap = load_ref[...] + table(0)
    res = pin_ref[...] + table(128)
    weight = weight_ref[...]
    iota8 = lax.broadcasted_iota(jnp.int32, (8, 2 * HALF), 0)
    tiles = NODES // 8
    cut = lambda a: [a[8 * t:8 * t + 8, :] for t in range(tiles)]
    sub, below, res = cut(cap), cut(weight), cut(res)
    for k in range(NODES - 1, 0, -1):
        t, r = divmod(k, 8)
        parent = jnp.broadcast_to(parent_ref[k:k + 1, :], iota8.shape)
        sub_k = jnp.broadcast_to(sub[t][r:r + 1, :], iota8.shape)
        below_k = jnp.broadcast_to(below[t][r:r + 1, :], iota8.shape)
        for a in range((k - 1) // 8 + 1):
            hit = parent == iota8 + 8 * a
            sub[a] = sub[a] + jnp.where(hit, sub_k, 0.0)
            below[a] = below[a] + jnp.where(hit, below_k, 0.0)
    step_d = [res[t] * sub[t] for t in range(tiles)]
    step_g = [res[t] * below[t] for t in range(tiles)]
    down_d, down_g = list(step_d), list(step_g)
    for k in range(1, NODES):
        t, r = divmod(k, 8)
        parent = jnp.broadcast_to(parent_ref[k:k + 1, :], iota8.shape)
        from_d = from_g = None
        for a in range((k - 1) // 8 + 1):
            hit = parent == iota8 + 8 * a
            d, g = jnp.where(hit, down_d[a], 0.0), jnp.where(hit, down_g[a], 0.0)
            from_d = d if from_d is None else from_d + d
            from_g = g if from_g is None else from_g + g
        here = iota8 == r
        down_d[t] = jnp.where(here, step_d[t] + jnp.sum(from_d, axis=0, keepdims=True), down_d[t])
        down_g[t] = jnp.where(here, step_g[t] + jnp.sum(from_g, axis=0, keepdims=True), down_g[t])
    delay_ref[...] = jnp.concatenate(down_d, axis=0)
    sens = jnp.concatenate(
        [SHEET * (below[t] * sub[t]) + GROUND * down_g[t] for t in range(tiles)], axis=0)
    high, low = split(sens)
    left_a[0:ROWS, 0:HALF] = jnp.concatenate(
        [high[:, :HALF], high[:, HALF:], low[:, :HALF], low[:, HALF:]], axis=0).astype(BF)
    iota_uf = lax.broadcasted_iota(jnp.int32, (64, CAPS), 0).astype(F32)

    def look_up(right, found):
        found[...] = mm(left_a[0:ROWS, 0:HALF], right[...], NN)

    def answer(u, found):
        upper = eight(upper_s, u)
        rows = []
        for j in range(8):
            both = found[:, j * CAPS:(j + 1) * CAPS]
            kept = jnp.where(iota_uf == upper[j:j + 1, :], both[:64] + both[64:], 0.0)
            rows.append(jnp.sum(kept, axis=0, keepdims=True))
        reply_ref[pl.ds(pl.multiple_of(u * 8, 8), 8), :] = jnp.concatenate(rows, axis=0)

    def answers(h, carry):
        look_up(right_b, found_b)
        answer(2 * h, found_a)
        build_right(jnp.minimum(2 * h + 2, units - 1), right_a)
        look_up(right_a, found_a)
        answer(2 * h + 1, found_b)
        build_right(jnp.minimum(2 * h + 3, units - 1), right_b)
        return carry

    look_up(right_a, found_a)
    lax.fori_loop(0, units // 2, answers, 0)


def final_kernel(returned_ref, owner_ref, rank_ref, out_ref, picks, ones_a, ones_b, found_a, found_b):
    high, low = split(returned_ref[...])
    picks[...] = jnp.concatenate([high, low], axis=0).astype(BF)
    iota_r = iota_bf(CAPS, 2 * SEG)
    iota_o = lax.broadcasted_iota(jnp.int32, (ROWS, 2 * SEG), 0)
    zero, one = jnp.zeros((), BF), jnp.ones((), BF)
    units = ROWS // 8

    def pair(rows, j):
        return jnp.concatenate([rows[2 * j:2 * j + 1, :], rows[2 * j + 1:2 * j + 2, :]], axis=1)

    def build(u, ones):
        rank = eight(rank_ref, u)
        for j in range(4):
            ones[:, j * 2 * SEG:(j + 1) * 2 * SEG] = jnp.where(
                iota_r == spread(pair(rank, j), CAPS), one, zero)

    def look_up(ones, found):
        found[...] = mm(picks[...], ones[...], NN)

    def answer(u, found):
        owner = eight(owner_ref, u)
        rows = []
        for j in range(4):
            both = found[:, j * 2 * SEG:(j + 1) * 2 * SEG]
            kept = jnp.where(iota_o == pair(owner, j), both[:ROWS] + both[ROWS:], 0.0)
            row = jnp.sum(kept, axis=0, keepdims=True)
            rows += [row[:, :SEG], row[:, SEG:]]
        out_ref[pl.ds(pl.multiple_of(u * 8, 8), 8), :] = jnp.concatenate(rows, axis=0)

    def two(h, carry):
        look_up(ones_b, found_b)
        answer(2 * h, found_a)
        build(jnp.minimum(2 * h + 2, units - 1), ones_a)
        look_up(ones_a, found_a)
        answer(2 * h + 1, found_b)
        build(jnp.minimum(2 * h + 3, units - 1), ones_b)
        return carry

    build(0, ones_a)
    build(1, ones_b)
    look_up(ones_a, found_a)
    lax.fori_loop(0, units // 2, two, 0)


def call(kernel, name, shapes, in_specs, scratch=()):
    vmem = pl.BlockSpec(memory_space=pltpu.VMEM)
    smem = pl.BlockSpec(memory_space=pltpu.SMEM)
    specs = [smem if c == "s" else vmem for c in in_specs]
    outs = [jax.ShapeDtypeStruct(shape, F32) for shape in shapes]
    single = len(outs) == 1
    return pl.pallas_call(
        kernel,
        out_shape=outs[0] if single else outs,
        in_specs=specs,
        out_specs=vmem if single else [vmem] * len(outs),
        scratch_shapes=[pltpu.VMEM(shape, dtype) for shape, dtype in scratch],
        compiler_params=pltpu.CompilerParams(vmem_limit_bytes=VMEM_LIMIT),
        name=name,
    )


def exchange(box):
    return lax.all_to_all(box, AXES, split_axis=0, concat_axis=0, tiled=True)


def body(seg_start, seg_len, seg_track, seg_nbr, seg_owner, seg_local, seg_node,
         pin_res, load_cap, crit_weight, net_parent):
    devices = lax.axis_size(AXES)
    forward = [(i, i + 1) for i in range(devices - 1)]
    backward = [(i + 1, i) for i in range(devices - 1)]
    feats = (seg_start, seg_len, seg_track)
    low = lax.ppermute(jnp.concatenate([f[-8:] for f in feats], axis=0), AXES, forward)
    high = lax.ppermute(jnp.concatenate([f[:8] for f in feats], axis=0), AXES, backward)
    owner = seg_owner.reshape(ROWS, SEG)
    square, flat = (ROWS, SEG), (ROWS, CAPS)
    rank = call(rank_kernel, "rank", [square], "v")(owner)
    first = (lax.axis_index(AXES) * ROWS).astype(jnp.int32).reshape(1)
    wide = (ROWS + 16, SEG)
    seg_cap, outbox = call(
        couple_kernel, "couple", [square, (ROWS, 3 * CAPS)], "ssvvvvvvvvv",
        [(wide, F32)] * 4 + [((SEG, 6 * SEG), BF), ((4 * SEG, SEG), BF)]
        + [((4 * SEG, 6 * SEG), F32)] * 2 + [((6 * ROWS, 8 * SEG), BF)] * 2
        + [((CAPS, 8 * SEG), BF)] * 2 + [((6 * ROWS, CAPS), F32)],
    )(first, seg_nbr, seg_start, seg_len, seg_track, low, high, owner, rank, seg_local, seg_node)
    inbox = exchange(outbox)
    delay, reply = call(
        owner_kernel, "owner", [(NODES, 2 * HALF), flat], "vvvvv",
        [(flat, F32), (flat, F32), ((4 * ROWS, CAPS), F32)] + [((CAPS, 8 * CAPS), BF)] * 4
        + [((ROWS, 8 * CAPS), F32)] * 2 + [((CAPS, HALF), F32)],
    )(inbox, pin_res, load_cap, crit_weight, net_parent)
    returned = exchange(reply)
    seg_sens = call(
        final_kernel, "final", [square], "vvv",
        [((2 * ROWS, CAPS), BF)] + [((CAPS, 8 * SEG), BF)] * 2 + [((2 * ROWS, 8 * SEG), F32)] * 2,
    )(returned, owner, rank)
    return seg_cap, delay, seg_sens


def solution(mesh):
    rows, nets = P(AXES, None), P(None, AXES)
    placed = (rows, rows, rows, rows, P(AXES, None, None), rows, rows, nets, nets, nets, nets)
    return jax.shard_map(body, mesh=mesh, in_specs=placed, out_specs=(rows, nets, rows), check_vma=False)
```

time: 171 us -> 98 us (0.57)
  Pallas kernels: 122 us -> 48.2 us
    pallas_call x3 -> x2, Pallas kernels: 96.7 us -> 30.7 us  [the longest x1 25.8 us: body(): call(couple_kernel, 'couple', [square, (ROWS, 3 * CAPS)], 'ssvvvvvvvvv',...]
    pallas_call x1, Pallas kernels: 20.4 us -> 12.8 us  [body(): call(owner_kernel, 'owner', [(NODES, 2 * HALF), flat], 'vvvvv', [(flat, F...]
  transfers between devices with their start and end apart: 2 -> 2, of which waited for: 0 -> 0; matrix products, arithmetic and copies ran while one was open for 0% -> 0% of each run, Pallas kernels for 3% -> 5%
where the time goes in v2:
time: 98 us; the launch traced here: 97.5 us
  Pallas kernels  48.2 us (49%)
  blocking collectives  36.1 us (37%)
  starting transfers between devices  7.82 us (8%)
  local copies, waits for them, and re-layouts  4.6 us (5%)
    all_to_all x2, blocking collectives, exchange(): return lax.all_to_all(box, AXES, split_axis=0, concat_axis=0, tiled=True)  36.1 us
    pallas_call x1, Pallas kernels, body(): call(couple_kernel, 'couple', [square, (ROWS, 3 * CAPS)], 'ssvvvvvvvvv',...  25.8 us
    pallas_call x1, Pallas kernels, body(): call(owner_kernel, 'owner', [(NODES, 2 * HALF), flat], 'vvvvv', [(flat, F...  12.8 us
    pallas_call x1, Pallas kernels, body(): call(final_kernel, 'final', [square], 'vvv', [((2 * ROWS, CAPS), BF)] + [...  4.85 us
    pallas_call x1, Pallas kernels, body(): rank = call(rank_kernel, 'rank', [square], 'v')(owner)  4.77 us
    ppermute x1, starting transfers between devices, body(): lax.ppermute(jnp.concatenate([f[-8:] for f in feats], axis=0), AXES, forw...  4.07 us
    ppermute x1, starting transfers between devices, body(): lax.ppermute(jnp.concatenate([f[:8] for f in feats], axis=0), AXES, backw...  3.75 us
    unnamed x25, local copies, waits for them, and re-layouts  2.58 us
  transfers between devices with their start and end apart: 2, of which 0 were waited for; matrix products, arithmetic and copies ran while one was open for 0% of the time, Pallas kernels for 5%

profile of v2, /device:TPU:1, one launch (start us, length us, event | category | flops | bytes accessed | tf_op | source)
XLA Modules:
  0.0 97.5 jit_solution(14139410266330780500)
XLA Ops:
  0.6 0.7 fusion.2
  1.4 0.7 fusion
  2.1 4.1 %collective-permute-start = (f32[24,128]{1,0:T(8,128)S(1)}, f32[24,128]{1,0:T(8,128)S(1)}, u32[]{:S(2)}, u32[]{:S(2)}) collective-permute-start(f32[24,128]{1,0:T(8,128)S(1)} %pad_maximum_fusion), channel_id=1, source_target_pairs={{0,1},{1,2},{2,3},{3,4},{4,5},{5,6},{6,7},{7,8},{8,9},{9,10},{10,1... | collective-permute-start | bytes 36872 | tf_op jit(solution)/shard_map/ppermute | solution.py:368
  6.2 3.7 %collective-permute-start.1 = (f32[24,128]{1,0:T(8,128)S(1)}, f32[24,128]{1,0:T(8,128)S(1)}, u32[]{:S(2)}, u32[]{:S(2)}) collective-permute-start(f32[24,128]{1,0:T(8,128)S(1)} %pad_maximum_fusion.1), channel_id=1, source_target_pairs={{1,0},{2,1},{3,2},{4,3},{5,4},{6,5},{7,6},{8,7},{9,8},{10,9},{11,1... | collective-permute-start | bytes 36872 | tf_op jit(solution)/shard_map/ppermute | solution.py:369
  10.0 0.0 copy-start.10
  10.0 0.0 copy-start.2
  10.0 0.0 copy-start.3
  10.0 4.8 %rank.1.rank_ref = f32[128,128]{1,0:T(8,128)S(1)} custom-call(s32[128,128]{1,0:T(8,128)S(1)} %bitcast.11), custom_call_target="tpu_custom_call" | custom-call | tf_op jit(solution)/shard_map/rank/pallas_call | solution.py:372
  14.8 0.0 copy-start.1
  14.8 0.1 copy.15.nbr_ref
  15.0 0.0 collective-permute-done.1.high_ref
  15.0 0.7 copy-done.1
  15.7 0.8 copy-done.5
  16.5 25.8 %couple.1 = (f32[128,128]{1,0:T(8,128)}, f32[128,768]{1,0:T(8,128)S(1)}) custom-call(s32[1]{0:T(128)} %bitcast.first_ref, s32[128,4]{1,0:T(8,128)S(1)} %copy.15.nbr_ref, f32[128,128]{1,0:T(8,128)S(1)} %copy-done.2, f32[128,128]{1,0:T(8,128)S(1)} %copy-done.3, f32[128,128]{1,0:T(8,128)S(1)} %copy-done.1, f32[24,128]{1,0:T(8,128)S(1)} %collective-permute-done.low_ref, ...), custom_call_target="tpu_custom_call" | custom-call | tf_op jit(solution)/shard_map/couple/pallas_call | solution.py:375
  42.3 0.4 copy.16
  42.7 22.2 %all_to_all.22 = f32[128,1,768]{2,1,0:T(1,128)S(1)} all-to-all(f32[128,1,768]{2,1,0:T(1,128)S(1)} %copy.16), channel_id=1, replica_groups=mesh['tile'=32,'net'=4] {'tile','net'}, dimensions={0} | all-to-all | bytes 786432 | tf_op jit(solution)/shard_map/all_to_all | solution.py:359
  65.0 0.8 copy-done.6
  65.8 0.0 copy-done.7
  65.8 0.0 copy-done.8
  65.8 0.0 copy-done.9
  65.9 12.8 %owner.1 = (f32[32,512]{1,0:T(8,128)}, f32[128,256]{1,0:T(8,128)S(1)}) custom-call(f32[128,768]{1,0:T(8,128)S(1)} %bitcast.10, f32[32,512]{1,0:T(8,128)S(1)} %copy-done.6, f32[32,512]{1,0:T(8,128)S(1)} %copy-done.7, f32[32,512]{1,0:T(8,128)S(1)} %copy-done.8, s32[32,512]{1,0:T(8,128)S(1)} %copy-done.9), custom_call_target="tpu_custom_call" | custom-call | tf_op jit(solution)/shard_map/owner/pallas_call | solution.py:382
  78.7 0.1 copy.17
  78.8 13.9 %all_to_all.23 = f32[128,1,256]{2,1,0:T(1,128)S(1)} all-to-all(f32[128,1,256]{2,1,0:T(1,128)S(1)} %copy.17), channel_id=1, replica_groups=mesh['tile'=32,'net'=4] {'tile','net'}, dimensions={0} | all-to-all | bytes 262144 | tf_op jit(solution)/shard_map/all_to_all | solution.py:359
  92.7 4.8 %final.1 = f32[128,128]{1,0:T(8,128)} custom-call(f32[128,256]{1,0:T(8,128)S(1)} %bitcast.14, s32[128,128]{1,0:T(8,128)S(1)} %bitcast.13, f32[128,128]{1,0:T(8,128)S(1)} %rank.1.rank_ref), custom_call_target="tpu_custom_call" | custom-call | tf_op jit(solution)/shard_map/final/pallas_call | solution.py:388
  (17 shorter events, 0.1 us)
Async XLA Ops:
  0.6 9.4 %copy-start = (s32[128,128,1]{1,2,0:T(1,128)S(1)}, s32[128,128,1]{1,2,0:T(1,128)}, u32[]{:S(2)}) copy-start(s32[128,128,1]{1,2,0:T(1,128)} %param.15) | copy-start | bytes 196612
  2.1 12.8 %copy-start.4 = (s32[128,128]{1,0:T(8,128)S(1)}, s32[128,128]{1,0:T(8,128)}, u32[]{:S(2)}) copy-start(s32[128,128]{1,0:T(8,128)} %local_ref.1) | copy-start | bytes 196612
  2.1 12.8 %collective-permute-start = (f32[24,128]{1,0:T(8,128)S(1)}, f32[24,128]{1,0:T(8,128)S(1)}, u32[]{:S(2)}, u32[]{:S(2)}) collective-permute-start(f32[24,128]{1,0:T(8,128)S(1)} %pad_maximum_fusion), channel_id=1, source_target_pairs={{0,1},{1,2},{2,3},{3,4},{4,5},{5,6},{6,7},{7,8},{8,9},{9,10},{10,1... | collective-permute-start | bytes 36872 | tf_op jit(solution)/shard_map/ppermute | solution.py:368
  6.2 8.7 %collective-permute-start.1 = (f32[24,128]{1,0:T(8,128)S(1)}, f32[24,128]{1,0:T(8,128)S(1)}, u32[]{:S(2)}, u32[]{:S(2)}) collective-permute-start(f32[24,128]{1,0:T(8,128)S(1)} %pad_maximum_fusion.1), channel_id=1, source_target_pairs={{1,0},{2,1},{3,2},{4,3},{5,4},{6,5},{7,6},{8,7},{9,8},{10,9},{11,1... | collective-permute-start | bytes 36872 | tf_op jit(solution)/shard_map/ppermute | solution.py:369
  10.0 4.8 %copy-start.10 = (s32[128,4]{0,1:T(4,128)S(1)}, s32[128,4]{0,1:T(4,128)}, u32[]{:S(2)}) copy-start(s32[128,4]{0,1:T(4,128)} %param.14) | copy-start | bytes 6148
  10.0 5.0 %copy-start.2 = (f32[128,128]{1,0:T(8,128)S(1)}, f32[128,128]{1,0:T(8,128)}, u32[]{:S(2)}) copy-start(f32[128,128]{1,0:T(8,128)} %start_ref.1) | copy-start | bytes 196612
  10.0 5.0 %copy-start.3 = (f32[128,128]{1,0:T(8,128)S(1)}, f32[128,128]{1,0:T(8,128)}, u32[]{:S(2)}) copy-start(f32[128,128]{1,0:T(8,128)} %len_ref.1) | copy-start | bytes 196612
  14.8 0.8 copy-start.1
  15.7 0.8 copy-start.5
  64.9 0.8 copy-start.6
  64.9 0.9 copy-start.7
  64.9 0.9 copy-start.8
  64.9 0.9 copy-start.9

commit v3 on v2

--- a/solution.py
+++ b/solution.py
@@ -20,6 +20,11 @@
 HALF = 256
 VMEM_LIMIT = 48 * 1024 * 1024
 
+RANK_ROWS = 64
+COUPLE_STEPS = 2
+OWNER_UNITS = 8
+FINAL_UNITS = 16
+
 NT = (((1,), (1,)), ((), ()))
 NN = (((1,), (0,)), ((), ()))
 
@@ -40,6 +45,18 @@
 def split(value):
     high = value.astype(BF).astype(F32)
     return high, (value - high).astype(BF).astype(F32)
+
+
+def repeat(count, together, step):
+    def several(h, carry):
+        for q in range(together):
+            step(h * together + q)
+        return carry
+
+    if count == together:
+        several(0, 0)
+    else:
+        lax.fori_loop(0, count // together, several, 0)
 
 
 def rank_kernel(owner_ref, rank_ref):
@@ -49,8 +66,8 @@
     upper = jnp.where((r0 <= c0), 1.0, 0.0).astype(BF)
 
     def step(g, before):
-        for j in range(8):
-            b = g * 8 + j
+        for j in range(RANK_ROWS):
+            b = g * RANK_ROWS + j
             hit = iota == owner_ref[pl.ds(b, 1), :]
             ones = jnp.where(hit, 1.0, 0.0).astype(BF)
             sums = mm(ones, upper, NN)
@@ -59,7 +76,7 @@
             before = before + sums[:, SEG:]
         return before
 
-    lax.fori_loop(0, ROWS // 8, step, jnp.zeros((ROWS, SEG), F32))
+    lax.fori_loop(0, ROWS // RANK_ROWS, step, jnp.zeros((ROWS, SEG), F32))
 
 
 def split3(value):
@@ -75,8 +92,7 @@
 
 def couple_kernel(first_ref, nbr_ref, start_ref, len_ref, track_ref, low_ref, high_ref,
                   owner_ref, rank_ref, local_ref, node_ref, cap_ref, out_ref,
-                  s_j, e_j, g_j, f_j, pick, shown, full_a, full_b,
-                  left_a, left_b, right_a, right_b, acc):
+                  s_j, e_j, g_j, f_j, pick, full_a, full_b, acc):
     def fill(at, count, start, length, track):
         s_j[at:at + count, :] = start
         e_j[at:at + count, :] = start + length
@@ -97,13 +113,15 @@
     zero, one = jnp.zeros((), BF), jnp.ones((), BF)
     first = first_ref[0]
 
-    def spread_columns(g, full):
+    def turn(g, full):
         at = pl.ds(pl.multiple_of(8 + g * 8, 8), 8)
         pieces = split3(s_j[at, :]) + split3(e_j[at, :]) + split3(g_j[at, :])
         turned = jnp.concatenate(pieces + [jnp.zeros((SEG - 72, SEG), F32)], axis=0).T
-        for pair in range(4):
-            shown[pair * SEG:(pair + 1) * SEG, :] = jnp.where(pair_of == pair, turned, 0.0).astype(BF)
-        full[...] = mm(shown[...], pick[...], NN)
+        full[...] = turned
+
+    def spread_pair(pair, full):
+        part = jnp.where(pair_of == pair, full[...], 0.0).astype(BF)
+        return mm(part, pick[...], NN)
 
     def pairs(g, j, full, sums):
         rows = []
@@ -114,7 +132,7 @@
             ])
         base = (j & 1) * 3 * SEG
         for t in range(SEG // 8):
-            part = slice((j >> 1) * SEG + 8 * t, (j >> 1) * SEG + 8 * t + 8)
+            part = slice(8 * t, 8 * t + 8)
             si = full[part, base:base + SEG]
             ei = full[part, base + SEG:base + 2 * SEG]
             gi = full[part, base + 2 * SEG:base + 3 * SEG]
@@ -129,58 +147,63 @@
         local, node = eight(local_ref, g), eight(node_ref, g)
         cap_hi, cap_lo = split(eight(cap_ref, g))
         res_hi, res_lo = split(SHEET * eight(len_ref, g))
-        upper = (local >> 8) * NODES + node
-        return [cap_hi, cap_lo, res_hi, res_lo,
-                (upper * HALF).astype(F32), (local & (HALF - 1)).astype(F32)]
-
-    def build(j, owner, rank, values, left, right):
-        lanes = slice(j * SEG, (j + 1) * SEG)
-        hit = iota_o == spread(owner[j:j + 1, :], ROWS)
-        for p in range(6):
-            value = spread(values[p][j:j + 1, :], ROWS)
-            left[p * ROWS:(p + 1) * ROWS, lanes] = jnp.where(hit, value, zero)
-        right[:, lanes] = jnp.where(iota_r == spread(rank[j:j + 1, :], CAPS), one, zero)
-
-    def step(g, full, full_next, left, right, left_old, right_old):
-        acc[...] += mm(left_old[...], right_old[...], NT)
-        spread_columns(jnp.minimum(g + 1, ROWS // 8 - 1), full_next)
+        slot = ((local >> 8) * NODES + node) * HALF + (local & (HALF - 1))
+        power = jnp.exp2(((slot >> 7) - 63).astype(F32))
+        return [cap_hi, cap_lo, res_hi, res_lo, power * (1.0 + (slot & 127).astype(F32) * (1.0 / 128))]
+
+    def send(j0, owner, rank, values):
+        cols = []
+        rows = []
+        for j in range(j0, j0 + 4):
+            hit = iota_o == spread(owner[j:j + 1, :], ROWS)
+            cols.append(jnp.concatenate(
+                [jnp.where(hit, spread(v[j:j + 1, :], ROWS), zero) for v in values], axis=0))
+            rows.append(jnp.where(iota_r == spread(rank[j:j + 1, :], CAPS), one, zero))
+        acc[...] += mm(jnp.concatenate(cols, axis=1), jnp.concatenate(rows, axis=1), NT)
+
+    def step(g, full, full_next):
+        turn(jnp.minimum(g + 1, ROWS // 8 - 1), full_next)
         last = jnp.maximum(g - 1, 0)
         owner = jnp.where(g > 0, eight(owner_ref, last).astype(F32), -1.0)
         rank, values = eight(rank_ref, last), values_of(last)
         sums = [jnp.zeros((8, SEG), F32)] * (SEG // 8)
         for j in range(8):
-            build(j, owner, rank, values, left, right)
-            pairs(g, j, full, sums)
+            if j % 4 == 0:
+                send(j, owner, rank, values)
+            if j % 2 == 0:
+                wide = spread_pair(j // 2, full)
+            pairs(g, j, wide, sums)
         summed = jnp.concatenate(sums, axis=0).T[:8, :]
         at = pl.ds(pl.multiple_of(g * 8, 8), 8)
         scale = f_j[pl.ds(pl.multiple_of(8 + g * 8, 8), 8), :]
         cap_ref[at, :] = GROUND * len_ref[at, :] + COUPLE * scale * summed
 
-    def two(h, carry):
-        step(2 * h, full_a, full_b, left_a, right_a, left_b, right_b)
-        step(2 * h + 1, full_b, full_a, left_b, right_b, left_a, right_a)
+    def several(h, carry):
+        for q in range(0, COUPLE_STEPS, 2):
+            step(COUPLE_STEPS * h + q, full_a, full_b)
+            step(COUPLE_STEPS * h + q + 1, full_b, full_a)
         return carry
 
     acc[...] = jnp.zeros_like(acc)
     cap_ref[0:8, :] = jnp.zeros((8, SEG), F32)
-    left_b[...] = jnp.zeros_like(left_b)
-    right_b[...] = jnp.zeros_like(right_b)
-    spread_columns(0, full_a)
-    lax.fori_loop(0, ROWS // 16, two, 0)
+    turn(0, full_a)
+    lax.fori_loop(0, ROWS // 8 // COUPLE_STEPS, several, 0)
     last = ROWS // 8 - 1
     owner, rank, values = eight(owner_ref, last).astype(F32), eight(rank_ref, last), values_of(last)
-    for j in range(8):
-        build(j, owner, rank, values, left_a, right_a)
-    acc[...] += mm(left_b[...], right_b[...], NT)
-    acc[...] += mm(left_a[...], right_a[...], NT)
-    for v in range(3):
+    for j in range(0, 8, 4):
+        send(j, owner, rank, values)
+    for v in range(2):
         high = acc[2 * v * ROWS:(2 * v + 1) * ROWS, :]
         low = acc[(2 * v + 1) * ROWS:(2 * v + 2) * ROWS, :]
         out_ref[:, v * CAPS:(v + 1) * CAPS] = high + low
+    coded = jnp.maximum(acc[4 * ROWS:5 * ROWS, :], 2.0 ** -63)
+    power = jnp.floor(jnp.log2(coded) + 63.002)
+    fraction = jnp.floor((coded * jnp.exp2(63.0 - power) - 1.0) * 128.0 + 0.5)
+    out_ref[:, 2 * CAPS:] = power * 128.0 + fraction
 
 
 def owner_kernel(inbox_ref, pin_ref, load_ref, weight_ref, parent_ref, delay_ref, reply_ref,
-                 upper_s, lower_s, pieces, left_a, left_b, right_a, right_b, found_a, found_b, acc):
+                 upper_s, lower_s, pieces, picks, acc):
     slot = inbox_ref[:, 2 * CAPS:].astype(jnp.int32)
     upper_s[...] = (slot >> 8).astype(F32)
     lower_s[...] = (slot & (HALF - 1)).astype(F32)
@@ -194,41 +217,27 @@
     zero, one = jnp.zeros((), BF), jnp.ones((), BF)
     units = ROWS // 8
 
-    def build_right(u, right):
-        lower = eight(lower_s, u)
-        for j in range(8):
-            right[:, j * CAPS:(j + 1) * CAPS] = jnp.where(
-                iota_l == spread(lower[j:j + 1, :], HALF), one, zero)
-
-    def build_left(u, left):
-        upper = eight(upper_s, u)
+    def lower_ones(lower, j):
+        return jnp.where(iota_l == spread(lower[j:j + 1, :], HALF), one, zero)
+
+    def collect(u):
+        upper, lower = eight(upper_s, u), eight(lower_s, u)
         values = [pieces[pl.ds(pl.multiple_of(p * ROWS + u * 8, 8), 8), :] for p in range(4)]
-        for j in range(8):
-            hit = iota_u == spread(upper[j:j + 1, :], 64)
-            for p in range(4):
-                left[p * 64:(p + 1) * 64, j * CAPS:(j + 1) * CAPS] = jnp.where(
-                    hit, spread(values[p][j:j + 1, :], 64), zero)
-
-    def collect(h, carry):
-        for u, now, later in (
-            (2 * h + 1, (left_a, right_a), (left_b, right_b)),
-            (jnp.minimum(2 * h + 2, units - 1), (left_b, right_b), (left_a, right_a)),
-        ):
-            acc[...] += mm(now[0][...], now[1][...], NT)
-            build_left(u, later[0])
-            build_right(u, later[1])
-        return carry
-
-    build_left(0, left_a)
-    build_right(0, right_a)
-    lax.fori_loop(0, units // 2, collect, 0)
+        for j0 in (0, 4):
+            left, right = [], []
+            for j in range(j0, j0 + 4):
+                hit = iota_u == spread(upper[j:j + 1, :], 64)
+                left.append(jnp.concatenate(
+                    [jnp.where(hit, spread(v[j:j + 1, :], 64), zero) for v in values], axis=0))
+                right.append(lower_ones(lower, j))
+            acc[...] += mm(jnp.concatenate(left, axis=1), jnp.concatenate(right, axis=1), NT)
+
+    repeat(units, OWNER_UNITS, collect)
 
     def table(at):
         both = acc[at:at + 64, :] + acc[at + 64:at + 128, :]
         return jnp.concatenate([both[:NODES], both[NODES:]], axis=1)
 
-    build_right(0, right_a)
-    build_right(1, right_b)
     cap = load_ref[...] + table(0)
     res = pin_ref[...] + table(128)
     weight = weight_ref[...]
@@ -264,78 +273,44 @@
     sens = jnp.concatenate(
         [SHEET * (below[t] * sub[t]) + GROUND * down_g[t] for t in range(tiles)], axis=0)
     high, low = split(sens)
-    left_a[0:ROWS, 0:HALF] = jnp.concatenate(
+    picks[...] = jnp.concatenate(
         [high[:, :HALF], high[:, HALF:], low[:, :HALF], low[:, HALF:]], axis=0).astype(BF)
     iota_uf = lax.broadcasted_iota(jnp.int32, (64, CAPS), 0).astype(F32)
 
-    def look_up(right, found):
-        found[...] = mm(left_a[0:ROWS, 0:HALF], right[...], NN)
-
-    def answer(u, found):
-        upper = eight(upper_s, u)
+    def answer(u):
+        upper, lower = eight(upper_s, u), eight(lower_s, u)
         rows = []
         for j in range(8):
-            both = found[:, j * CAPS:(j + 1) * CAPS]
+            both = mm(picks[...], lower_ones(lower, j), NN)
             kept = jnp.where(iota_uf == upper[j:j + 1, :], both[:64] + both[64:], 0.0)
             rows.append(jnp.sum(kept, axis=0, keepdims=True))
         reply_ref[pl.ds(pl.multiple_of(u * 8, 8), 8), :] = jnp.concatenate(rows, axis=0)
 
-    def answers(h, carry):
-        look_up(right_b, found_b)
-        answer(2 * h, found_a)
-        build_right(jnp.minimum(2 * h + 2, units - 1), right_a)
-        look_up(right_a, found_a)
-        answer(2 * h + 1, found_b)
-        build_right(jnp.minimum(2 * h + 3, units - 1), right_b)
-        return carry
-
-    look_up(right_a, found_a)
-    lax.fori_loop(0, units // 2, answers, 0)
-
-
-def final_kernel(returned_ref, owner_ref, rank_ref, out_ref, picks, ones_a, ones_b, found_a, found_b):
+    repeat(units, OWNER_UNITS, answer)
+
+
+def final_kernel(returned_ref, owner_ref, rank_ref, out_ref, picks):
     high, low = split(returned_ref[...])
     picks[...] = jnp.concatenate([high, low], axis=0).astype(BF)
     iota_r = iota_bf(CAPS, 2 * SEG)
     iota_o = lax.broadcasted_iota(jnp.int32, (ROWS, 2 * SEG), 0)
     zero, one = jnp.zeros((), BF), jnp.ones((), BF)
-    units = ROWS // 8
 
     def pair(rows, j):
         return jnp.concatenate([rows[2 * j:2 * j + 1, :], rows[2 * j + 1:2 * j + 2, :]], axis=1)
 
-    def build(u, ones):
-        rank = eight(rank_ref, u)
-        for j in range(4):
-            ones[:, j * 2 * SEG:(j + 1) * 2 * SEG] = jnp.where(
-                iota_r == spread(pair(rank, j), CAPS), one, zero)
-
-    def look_up(ones, found):
-        found[...] = mm(picks[...], ones[...], NN)
-
-    def answer(u, found):
-        owner = eight(owner_ref, u)
+    def answer(u):
+        rank, owner = eight(rank_ref, u), eight(owner_ref, u)
         rows = []
         for j in range(4):
-            both = found[:, j * 2 * SEG:(j + 1) * 2 * SEG]
+            ones = jnp.where(iota_r == spread(pair(rank, j), CAPS), one, zero)
+            both = mm(picks[...], ones, NN)
             kept = jnp.where(iota_o == pair(owner, j), both[:ROWS] + both[ROWS:], 0.0)
             row = jnp.sum(kept, axis=0, keepdims=True)
             rows += [row[:, :SEG], row[:, SEG:]]
         out_ref[pl.ds(pl.multiple_of(u * 8, 8), 8), :] = jnp.concatenate(rows, axis=0)
 
-    def two(h, carry):
-        look_up(ones_b, found_b)
-        answer(2 * h, found_a)
-        build(jnp.minimum(2 * h + 2, units - 1), ones_a)
-        look_up(ones_a, found_a)
-        answer(2 * h + 1, found_b)
-        build(jnp.minimum(2 * h + 3, units - 1), ones_b)
-        return carry
-
-    build(0, ones_a)
-    build(1, ones_b)
-    look_up(ones_a, found_a)
-    lax.fori_loop(0, units // 2, two, 0)
+    repeat(ROWS // 8, FINAL_UNITS, answer)
 
 
 def call(kernel, name, shapes, in_specs, scratch=()):
@@ -374,20 +349,17 @@
     wide = (ROWS + 16, SEG)
     seg_cap, outbox = call(
         couple_kernel, "couple", [square, (ROWS, 3 * CAPS)], "ssvvvvvvvvv",
-        [(wide, F32)] * 4 + [((SEG, 6 * SEG), BF), ((4 * SEG, SEG), BF)]
-        + [((4 * SEG, 6 * SEG), F32)] * 2 + [((6 * ROWS, 8 * SEG), BF)] * 2
-        + [((CAPS, 8 * SEG), BF)] * 2 + [((6 * ROWS, CAPS), F32)],
+        [(wide, F32)] * 4 + [((SEG, 6 * SEG), BF)] + [(square, F32)] * 2 + [((5 * ROWS, CAPS), F32)],
     )(first, seg_nbr, seg_start, seg_len, seg_track, low, high, owner, rank, seg_local, seg_node)
     inbox = exchange(outbox)
     delay, reply = call(
         owner_kernel, "owner", [(NODES, 2 * HALF), flat], "vvvvv",
-        [(flat, F32), (flat, F32), ((4 * ROWS, CAPS), F32)] + [((CAPS, 8 * CAPS), BF)] * 4
-        + [((ROWS, 8 * CAPS), F32)] * 2 + [((CAPS, HALF), F32)],
+        [(flat, F32), (flat, F32), ((4 * ROWS, CAPS), F32), ((ROWS, HALF), BF), ((CAPS, HALF), F32)],
     )(inbox, pin_res, load_cap, crit_weight, net_parent)
     returned = exchange(reply)
     seg_sens = call(
         final_kernel, "final", [square], "vvv",
-        [((2 * ROWS, CAPS), BF)] + [((CAPS, 8 * SEG), BF)] * 2 + [((2 * ROWS, 8 * SEG), F32)] * 2,
+        [((2 * ROWS, CAPS), BF)],
     )(returned, owner, rank)
     return seg_cap, delay, seg_sens
 

time: 98 us -> 86.2 us (0.88)
  Pallas kernels: 48.2 us -> 35.6 us
    pallas_call x1, Pallas kernels: 25.8 us -> 21 us  [body(): call(couple_kernel, 'couple', [square, (ROWS, 3 * CAPS)], 'ssvvvvvvvvv',...]
    pallas_call x1, Pallas kernels: 12.8 us -> 8.54 us  [body(): call(owner_kernel, 'owner', [(NODES, 2 * HALF), flat], 'vvvvv', [(flat, F...]
    pallas_call x1, Pallas kernels: 4.77 us -> 2.77 us  [body(): rank = call(rank_kernel, 'rank', [square], 'v')(owner)]
    pallas_call x1, Pallas kernels: 4.85 us -> 3.26 us  [body(): call(final_kernel, 'final', [square], 'vvv', [((2 * ROWS, CAPS), BF)])]
  transfers between devices with their start and end apart: 2 -> 2, of which waited for: 0 -> 0; matrix products, arithmetic and copies ran while one was open for 0% -> 0% of each run, Pallas kernels for 5% -> 3%
where the time goes in v3:
time: 86.2 us; the launch traced here: 85.8 us
  blocking collectives  37 us (43%)
  Pallas kernels  35.6 us (41%)
  starting transfers between devices  7.82 us (9%)
  local copies, waits for them, and re-layouts  4.6 us (5%)
    all_to_all x2, blocking collectives, exchange(): return lax.all_to_all(box, AXES, split_axis=0, concat_axis=0, tiled=True)  37 us
    pallas_call x1, Pallas kernels, body(): call(couple_kernel, 'couple', [square, (ROWS, 3 * CAPS)], 'ssvvvvvvvvv',...  21 us
    pallas_call x1, Pallas kernels, body(): call(owner_kernel, 'owner', [(NODES, 2 * HALF), flat], 'vvvvv', [(flat, F...  8.54 us
    ppermute x1, starting transfers between devices, body(): lax.ppermute(jnp.concatenate([f[-8:] for f in feats], axis=0), AXES, forw...  4.07 us
    ppermute x1, starting transfers between devices, body(): lax.ppermute(jnp.concatenate([f[:8] for f in feats], axis=0), AXES, backw...  3.75 us
    pallas_call x1, Pallas kernels, body(): call(final_kernel, 'final', [square], 'vvv', [((2 * ROWS, CAPS), BF)])  3.26 us
    pallas_call x1, Pallas kernels, body(): rank = call(rank_kernel, 'rank', [square], 'v')(owner)  2.77 us
    unnamed x25, local copies, waits for them, and re-layouts  2.58 us
  transfers between devices with their start and end apart: 2, of which 0 were waited for; matrix products, arithmetic and copies ran while one was open for 0% of the time, Pallas kernels for 3%

profile of v3, /device:TPU:1, one launch (start us, length us, event | category | flops | bytes accessed | tf_op | source)
XLA Modules:
  0.0 85.8 jit_solution(2140938910239556325)
XLA Ops:
  0.6 0.7 fusion.2
  1.4 0.7 fusion
  2.1 4.1 %collective-permute-start = (f32[24,128]{1,0:T(8,128)S(1)}, f32[24,128]{1,0:T(8,128)S(1)}, u32[]{:S(2)}, u32[]{:S(2)}) collective-permute-start(f32[24,128]{1,0:T(8,128)S(1)} %pad_maximum_fusion), channel_id=1, source_target_pairs={{0,1},{1,2},{2,3},{3,4},{4,5},{5,6},{6,7},{7,8},{8,9},{9,10},{10,1... | collective-permute-start | bytes 36872 | tf_op jit(solution)/shard_map/ppermute | solution.py:343
  6.2 3.7 %collective-permute-start.1 = (f32[24,128]{1,0:T(8,128)S(1)}, f32[24,128]{1,0:T(8,128)S(1)}, u32[]{:S(2)}, u32[]{:S(2)}) collective-permute-start(f32[24,128]{1,0:T(8,128)S(1)} %pad_maximum_fusion.1), channel_id=1, source_target_pairs={{1,0},{2,1},{3,2},{4,3},{5,4},{6,5},{7,6},{8,7},{9,8},{10,9},{11,1... | collective-permute-start | bytes 36872 | tf_op jit(solution)/shard_map/ppermute | solution.py:344
  10.0 0.0 copy-start.10
  10.0 0.0 copy-start.2
  10.0 0.0 copy-start.3
  10.0 2.8 %rank.1.rank_ref = f32[128,128]{1,0:T(8,128)S(1)} custom-call(s32[128,128]{1,0:T(8,128)S(1)} %bitcast.11), custom_call_target="tpu_custom_call" | custom-call | tf_op jit(solution)/shard_map/rank/pallas_call | solution.py:347
  12.8 0.0 copy-start.1
  12.8 0.1 copy.15.nbr_ref
  12.9 0.0 collective-permute-done.low_ref
  13.0 0.7 copy-done.1
  13.7 0.8 copy-done.5
  14.5 21.0 %couple.1 = (f32[128,128]{1,0:T(8,128)}, f32[128,768]{1,0:T(8,128)S(1)}) custom-call(s32[1]{0:T(128)} %bitcast.first_ref, s32[128,4]{1,0:T(8,128)S(1)} %copy.15.nbr_ref, f32[128,128]{1,0:T(8,128)S(1)} %copy-done.2, f32[128,128]{1,0:T(8,128)S(1)} %copy-done.3, f32[128,128]{1,0:T(8,128)S(1)} %copy-done.1, f32[24,128]{1,0:T(8,128)S(1)} %collective-permute-done.low_ref, ...), custom_call_target="tpu_custom_call" | custom-call | tf_op jit(solution)/shard_map/couple/pallas_call | solution.py:350
  35.5 0.4 copy.16
  35.9 23.1 %all_to_all.22 = f32[128,1,768]{2,1,0:T(1,128)S(1)} all-to-all(f32[128,1,768]{2,1,0:T(1,128)S(1)} %copy.16), channel_id=1, replica_groups=mesh['tile'=32,'net'=4] {'tile','net'}, dimensions={0} | all-to-all | bytes 786432 | tf_op jit(solution)/shard_map/all_to_all | solution.py:334
  59.1 0.8 copy-done.6
  59.9 0.0 copy-done.7
  59.9 0.0 copy-done.8
  59.9 0.0 copy-done.9
  60.0 8.5 %owner.1 = (f32[32,512]{1,0:T(8,128)}, f32[128,256]{1,0:T(8,128)S(1)}) custom-call(f32[128,768]{1,0:T(8,128)S(1)} %bitcast.10, f32[32,512]{1,0:T(8,128)S(1)} %copy-done.6, f32[32,512]{1,0:T(8,128)S(1)} %copy-done.7, f32[32,512]{1,0:T(8,128)S(1)} %copy-done.8, s32[32,512]{1,0:T(8,128)S(1)} %copy-done.9), custom_call_target="tpu_custom_call" | custom-call | tf_op jit(solution)/shard_map/owner/pallas_call | solution.py:355
  68.5 0.1 copy.17
  68.6 13.9 %all_to_all.23 = f32[128,1,256]{2,1,0:T(1,128)S(1)} all-to-all(f32[128,1,256]{2,1,0:T(1,128)S(1)} %copy.17), channel_id=1, replica_groups=mesh['tile'=32,'net'=4] {'tile','net'}, dimensions={0} | all-to-all | bytes 262144 | tf_op jit(solution)/shard_map/all_to_all | solution.py:334
  82.5 3.3 %final.1 = f32[128,128]{1,0:T(8,128)} custom-call(f32[128,256]{1,0:T(8,128)S(1)} %bitcast.14, s32[128,128]{1,0:T(8,128)S(1)} %bitcast.13, f32[128,128]{1,0:T(8,128)S(1)} %rank.1.rank_ref), custom_call_target="tpu_custom_call" | custom-call | tf_op jit(solution)/shard_map/final/pallas_call | solution.py:360
  (17 shorter events, 0.1 us)
Async XLA Ops:
  0.6 9.4 %copy-start = (s32[128,128,1]{1,2,0:T(1,128)S(1)}, s32[128,128,1]{1,2,0:T(1,128)}, u32[]{:S(2)}) copy-start(s32[128,128,1]{1,2,0:T(1,128)} %param.15) | copy-start | bytes 196612
  2.1 10.8 %copy-start.4 = (s32[128,128]{1,0:T(8,128)S(1)}, s32[128,128]{1,0:T(8,128)}, u32[]{:S(2)}) copy-start(s32[128,128]{1,0:T(8,128)} %local_ref.1) | copy-start | bytes 196612
  2.1 10.8 %collective-permute-start = (f32[24,128]{1,0:T(8,128)S(1)}, f32[24,128]{1,0:T(8,128)S(1)}, u32[]{:S(2)}, u32[]{:S(2)}) collective-permute-start(f32[24,128]{1,0:T(8,128)S(1)} %pad_maximum_fusion), channel_id=1, source_target_pairs={{0,1},{1,2},{2,3},{3,4},{4,5},{5,6},{6,7},{7,8},{8,9},{9,10},{10,1... | collective-permute-start | bytes 36872 | tf_op jit(solution)/shard_map/ppermute | solution.py:343
  6.2 6.7 %collective-permute-start.1 = (f32[24,128]{1,0:T(8,128)S(1)}, f32[24,128]{1,0:T(8,128)S(1)}, u32[]{:S(2)}, u32[]{:S(2)}) collective-permute-start(f32[24,128]{1,0:T(8,128)S(1)} %pad_maximum_fusion.1), channel_id=1, source_target_pairs={{1,0},{2,1},{3,2},{4,3},{5,4},{6,5},{7,6},{8,7},{9,8},{10,9},{11,1... | collective-permute-start | bytes 36872 | tf_op jit(solution)/shard_map/ppermute | solution.py:344
  10.0 2.8 %copy-start.10 = (s32[128,4]{0,1:T(4,128)S(1)}, s32[128,4]{0,1:T(4,128)}, u32[]{:S(2)}) copy-start(s32[128,4]{0,1:T(4,128)} %param.14) | copy-start | bytes 6148
  10.0 3.0 %copy-start.2 = (f32[128,128]{1,0:T(8,128)S(1)}, f32[128,128]{1,0:T(8,128)}, u32[]{:S(2)}) copy-start(f32[128,128]{1,0:T(8,128)} %start_ref.1) | copy-start | bytes 196612
  10.0 3.0 %copy-start.3 = (f32[128,128]{1,0:T(8,128)S(1)}, f32[128,128]{1,0:T(8,128)}, u32[]{:S(2)}) copy-start(f32[128,128]{1,0:T(8,128)} %len_ref.1) | copy-start | bytes 196612
  12.8 0.8 copy-start.1
  13.7 0.8 copy-start.5
  59.0 0.8 copy-start.6
  59.0 0.9 %copy-start.7 = (f32[32,512]{1,0:T(8,128)S(1)}, f32[32,512]{1,0:T(8,128)}, u32[]{:S(2)}) copy-start(f32[32,512]{1,0:T(8,128)} %load_ref.1) | copy-start | bytes 196612
  59.0 0.9 %copy-start.8 = (f32[32,512]{1,0:T(8,128)S(1)}, f32[32,512]{1,0:T(8,128)}, u32[]{:S(2)}) copy-start(f32[32,512]{1,0:T(8,128)} %weight_ref.1) | copy-start | bytes 196612
  59.0 0.9 %copy-start.9 = (s32[32,512]{1,0:T(8,128)S(1)}, s32[32,512]{1,0:T(8,128)}, u32[]{:S(2)}) copy-start(s32[32,512]{1,0:T(8,128)} %parent_ref.1) | copy-start | bytes 196612

commit v4 on v3

--- a/solution.py
+++ b/solution.py
@@ -18,7 +18,7 @@
 CAPS = 256
 NODES = 32
 HALF = 256
-VMEM_LIMIT = 48 * 1024 * 1024
+VMEM_LIMIT = 24 * 1024 * 1024
 
 RANK_ROWS = 64
 COUPLE_STEPS = 2
@@ -57,6 +57,29 @@
         several(0, 0)
     else:
         lax.fori_loop(0, count // together, several, 0)
+
+
+def even_device(first_ref):
+    return ((first_ref[0] // ROWS) & 1) == 0
+
+
+def copy_all(pairs, sems):
+    copies = [pltpu.make_async_copy(source, target, sems.at[n]) for n, (source, target) in enumerate(pairs)]
+    for copy in copies:
+        copy.start()
+    return copies
+
+
+def edge_kernel(first_ref, start_hbm, len_hbm, track_hbm, near_ref, far_ref, sems):
+    even = even_device(first_ref)
+    high = pl.multiple_of(jnp.where(even, ROWS - 8, 0), 8)
+    low = pl.multiple_of(jnp.where(even, 0, ROWS - 8), 8)
+    pairs = []
+    for n, source in enumerate((start_hbm, len_hbm, track_hbm)):
+        pairs.append((source.at[pl.ds(low, 8), :], far_ref.at[8 * n:8 * n + 8, :]))
+        pairs.append((source.at[pl.ds(high, 8), :], near_ref.at[8 * n:8 * n + 8, :]))
+    for copy in copy_all(pairs, sems):
+        copy.wait()
 
 
 def rank_kernel(owner_ref, rank_ref):
@@ -90,7 +113,20 @@
     return ref[pl.ds(pl.multiple_of(group * 8, 8), 8), :]
 
 
-def couple_kernel(first_ref, nbr_ref, start_ref, len_ref, track_ref, low_ref, high_ref,
+def lines(value, half, width):
+    return pl.ds(2 * value + half, ROWS, stride=width)
+
+
+def place(ref, value, array):
+    for half in (0, 1):
+        ref[lines(value, half, 6), :] = array[:, half * SEG:(half + 1) * SEG]
+
+
+def take(ref, value, width):
+    return jnp.concatenate([ref[lines(value, half, width), :] for half in (0, 1)], axis=1)
+
+
+def couple_kernel(first_ref, nbr_ref, start_ref, len_ref, track_ref, near_ref, far_ref,
                   owner_ref, rank_ref, local_ref, node_ref, cap_ref, out_ref,
                   s_j, e_j, g_j, f_j, pick, full_a, full_b, acc):
     def fill(at, count, start, length, track):
@@ -100,8 +136,10 @@
         f_j[at:at + count, :] = jnp.exp(-track)
 
     fill(8, ROWS, start_ref[...], len_ref[...], track_ref[...])
-    fill(0, 8, low_ref[0:8, :], low_ref[8:16, :], low_ref[16:24, :])
-    fill(8 + ROWS, 8, high_ref[0:8, :], high_ref[8:16, :], high_ref[16:24, :])
+    even, near, far = even_device(first_ref), near_ref[...], far_ref[...]
+    low, high = jnp.where(even, far, near), jnp.where(even, near, far)
+    fill(0, 8, low[0:8, :], low[8:16, :], low[16:24, :])
+    fill(8 + ROWS, 8, high[0:8, :], high[8:16, :], high[16:24, :])
     row = lax.broadcasted_iota(jnp.int32, (SEG, 6 * SEG), 0)
     col = lax.broadcasted_iota(jnp.int32, (SEG, 6 * SEG), 1) >> 7
     array = jnp.where(row < 24, 0, jnp.where(row < 48, 1, jnp.where(row < 72, 2, 9)))
@@ -126,7 +164,7 @@
     def pairs(g, j, full, sums):
         rows = []
         for k in range(4):
-            near = jnp.clip(nbr_ref[g * 8 + j, k] - first + 8, 0, ROWS + 15)
+            near = jnp.clip(nbr_ref[k, g * 8 + j] - first + 8, 0, ROWS + 15)
             rows.append([
                 jnp.broadcast_to(ref[pl.ds(near, 1), :], (8, SEG)) for ref in (s_j, e_j, g_j, f_j)
             ])
@@ -195,20 +233,22 @@
     for v in range(2):
         high = acc[2 * v * ROWS:(2 * v + 1) * ROWS, :]
         low = acc[(2 * v + 1) * ROWS:(2 * v + 2) * ROWS, :]
-        out_ref[:, v * CAPS:(v + 1) * CAPS] = high + low
+        place(out_ref, v, high + low)
     coded = jnp.maximum(acc[4 * ROWS:5 * ROWS, :], 2.0 ** -63)
     power = jnp.floor(jnp.log2(coded) + 63.002)
     fraction = jnp.floor((coded * jnp.exp2(63.0 - power) - 1.0) * 128.0 + 0.5)
-    out_ref[:, 2 * CAPS:] = power * 128.0 + fraction
-
-
-def owner_kernel(inbox_ref, pin_ref, load_ref, weight_ref, parent_ref, delay_ref, reply_ref,
-                 upper_s, lower_s, pieces, picks, acc):
-    slot = inbox_ref[:, 2 * CAPS:].astype(jnp.int32)
+    place(out_ref, 2, power * 128.0 + fraction)
+
+
+def owner_kernel(inbox_ref, pin_hbm, load_hbm, weight_hbm, parent_hbm, delay_ref, reply_ref,
+                 upper_s, lower_s, pieces, picks, acc, pin_ref, load_ref, weight_ref, parent_ref, sems):
+    copies = copy_all(((pin_hbm, pin_ref), (load_hbm, load_ref), (weight_hbm, weight_ref),
+                       (parent_hbm, parent_ref)), sems)
+    slot = take(inbox_ref, 2, 6).astype(jnp.int32)
     upper_s[...] = (slot >> 8).astype(F32)
     lower_s[...] = (slot & (HALF - 1)).astype(F32)
     for v in range(2):
-        high, low = split(inbox_ref[:, v * CAPS:(v + 1) * CAPS])
+        high, low = split(take(inbox_ref, v, 6))
         pieces[2 * v * ROWS:(2 * v + 1) * ROWS, :] = high
         pieces[(2 * v + 1) * ROWS:(2 * v + 2) * ROWS, :] = low
     acc[...] = jnp.zeros_like(acc)
@@ -233,6 +273,8 @@
             acc[...] += mm(jnp.concatenate(left, axis=1), jnp.concatenate(right, axis=1), NT)
 
     repeat(units, OWNER_UNITS, collect)
+    for copy in copies:
+        copy.wait()
 
     def table(at):
         both = acc[at:at + 64, :] + acc[at + 64:at + 128, :]
@@ -284,13 +326,15 @@
             both = mm(picks[...], lower_ones(lower, j), NN)
             kept = jnp.where(iota_uf == upper[j:j + 1, :], both[:64] + both[64:], 0.0)
             rows.append(jnp.sum(kept, axis=0, keepdims=True))
-        reply_ref[pl.ds(pl.multiple_of(u * 8, 8), 8), :] = jnp.concatenate(rows, axis=0)
+        reply = jnp.concatenate(rows, axis=0)
+        for half in (0, 1):
+            reply_ref[pl.ds(u * 16 + half, 8, stride=2), :] = reply[:, half * SEG:(half + 1) * SEG]
 
     repeat(units, OWNER_UNITS, answer)
 
 
 def final_kernel(returned_ref, owner_ref, rank_ref, out_ref, picks):
-    high, low = split(returned_ref[...])
+    high, low = split(take(returned_ref, 0, 2))
     picks[...] = jnp.concatenate([high, low], axis=0).astype(BF)
     iota_r = iota_bf(CAPS, 2 * SEG)
     iota_o = lax.broadcasted_iota(jnp.int32, (ROWS, 2 * SEG), 0)
@@ -313,54 +357,58 @@
     repeat(ROWS // 8, FINAL_UNITS, answer)
 
 
-def call(kernel, name, shapes, in_specs, scratch=()):
-    vmem = pl.BlockSpec(memory_space=pltpu.VMEM)
-    smem = pl.BlockSpec(memory_space=pltpu.SMEM)
-    specs = [smem if c == "s" else vmem for c in in_specs]
-    outs = [jax.ShapeDtypeStruct(shape, F32) for shape in shapes]
-    single = len(outs) == 1
+def call(kernel, name, outs, in_specs, scratch=(), copies=0, cost=None, limit=VMEM_LIMIT):
+    spaces = {"s": pltpu.SMEM, "v": pltpu.VMEM, "h": pltpu.HBM}
+    specs = [pl.BlockSpec(memory_space=spaces[letter]) for letter in in_specs]
+    scratch_shapes = [pltpu.VMEM(shape, dtype) for shape, dtype in scratch]
+    if copies:
+        scratch_shapes.append(pltpu.SemaphoreType.DMA((copies,)))
     return pl.pallas_call(
         kernel,
-        out_shape=outs[0] if single else outs,
+        out_shape=[jax.ShapeDtypeStruct(out, F32) for out in outs],
         in_specs=specs,
-        out_specs=vmem if single else [vmem] * len(outs),
-        scratch_shapes=[pltpu.VMEM(shape, dtype) for shape, dtype in scratch],
-        compiler_params=pltpu.CompilerParams(vmem_limit_bytes=VMEM_LIMIT),
+        out_specs=[pl.BlockSpec(memory_space=pltpu.VMEM)] * len(outs),
+        scratch_shapes=scratch_shapes,
+        compiler_params=pltpu.CompilerParams(vmem_limit_bytes=limit),
+        cost_estimate=cost and pl.CostEstimate(flops=cost * 10 ** 9, bytes_accessed=0, transcendentals=0),
         name=name,
     )
 
 
-def exchange(box):
-    return lax.all_to_all(box, AXES, split_axis=0, concat_axis=0, tiled=True)
+def exchange(lines_of):
+    box = lines_of.reshape(ROWS, 1, -1)
+    return lax.all_to_all(box, AXES, split_axis=0, concat_axis=0, tiled=True).reshape(lines_of.shape)
 
 
 def body(seg_start, seg_len, seg_track, seg_nbr, seg_owner, seg_local, seg_node,
          pin_res, load_cap, crit_weight, net_parent):
     devices = lax.axis_size(AXES)
-    forward = [(i, i + 1) for i in range(devices - 1)]
-    backward = [(i + 1, i) for i in range(devices - 1)]
-    feats = (seg_start, seg_len, seg_track)
-    low = lax.ppermute(jnp.concatenate([f[-8:] for f in feats], axis=0), AXES, forward)
-    high = lax.ppermute(jnp.concatenate([f[:8] for f in feats], axis=0), AXES, backward)
+    in_pair = [(i, i ^ 1) for i in range(devices)]
+    between = [(i, i + 1 if i % 2 else i - 1) for i in range(1, devices - 1)]
+    I32 = jnp.int32
     owner = seg_owner.reshape(ROWS, SEG)
-    square, flat = (ROWS, SEG), (ROWS, CAPS)
-    rank = call(rank_kernel, "rank", [square], "v")(owner)
-    first = (lax.axis_index(AXES) * ROWS).astype(jnp.int32).reshape(1)
+    square, flat, nets = (ROWS, SEG), (ROWS, CAPS), (NODES, 2 * HALF)
+    first = (lax.axis_index(AXES) * ROWS).astype(I32).reshape(1)
+    near, far = call(edge_kernel, "edge", [(24, SEG)] * 2, "shhh", copies=6, limit=None)(
+        first, seg_start, seg_len, seg_track)
+    far = lax.ppermute(far, AXES, between)
+    near = lax.ppermute(near, AXES, in_pair)
+    rank, = call(rank_kernel, "rank", [square], "v", cost=3)(owner)
     wide = (ROWS + 16, SEG)
     seg_cap, outbox = call(
-        couple_kernel, "couple", [square, (ROWS, 3 * CAPS)], "ssvvvvvvvvv",
+        couple_kernel, "couple", [square, (6 * ROWS, SEG)], "ssvvvvvvvvv",
         [(wide, F32)] * 4 + [((SEG, 6 * SEG), BF)] + [(square, F32)] * 2 + [((5 * ROWS, CAPS), F32)],
-    )(first, seg_nbr, seg_start, seg_len, seg_track, low, high, owner, rank, seg_local, seg_node)
+        cost=20,
+    )(first, seg_nbr.T, seg_start, seg_len, seg_track, near, far, owner, rank, seg_local, seg_node)
     inbox = exchange(outbox)
     delay, reply = call(
-        owner_kernel, "owner", [(NODES, 2 * HALF), flat], "vvvvv",
-        [(flat, F32), (flat, F32), ((4 * ROWS, CAPS), F32), ((ROWS, HALF), BF), ((CAPS, HALF), F32)],
+        owner_kernel, "owner", [nets, (2 * ROWS, SEG)], "vhhhh",
+        [(flat, F32), (flat, F32), ((4 * ROWS, CAPS), F32), ((ROWS, HALF), BF), ((CAPS, HALF), F32)]
+        + [(nets, F32)] * 3 + [(nets, I32)], copies=4, cost=9,
     )(inbox, pin_res, load_cap, crit_weight, net_parent)
     returned = exchange(reply)
-    seg_sens = call(
-        final_kernel, "final", [square], "vvv",
-        [((2 * ROWS, CAPS), BF)],
-    )(returned, owner, rank)
+    seg_sens, = call(final_kernel, "final", [square], "vvv", [((2 * ROWS, CAPS), BF)], cost=3)(
+        returned, owner, rank)
     return seg_cap, delay, seg_sens
 
 

time: 86.2 us -> 81.5 us (0.945)
  local copies, waits for them, and re-layouts: 4.6 us -> 0.06 us
  starting transfers between devices: 7.82 us -> 6.67 us
    unnamed x25 -> x22, local copies, waits for them, and re-layouts: 2.58 us -> 0.06 us
    slice x2 -> x0, local copies, waits for them, and re-layouts: 1.48 us -> none  [body(): f[:8]]
    ppermute x2, starting transfers between devices: 7.82 us -> 6.67 us  [the longest x1 4.55 us: body(): far = lax.ppermute(far, AXES, between)]
    pallas_call x4 -> x5, Pallas kernels: 35.6 us -> 36.2 us  [the longest x1 19.9 us: body(): call(couple_kernel, 'couple', [square, (6 * ROWS, SEG)], 'ssvvvvvvvvv', [...]
where the time goes in v4:
time: 81.5 us; the launch traced here: 81.3 us
  blocking collectives  37.6 us (46%)
  Pallas kernels  36.2 us (44%)
  starting transfers between devices  6.67 us (8%)
    all_to_all x2, blocking collectives, exchange(): lax.all_to_all(box, AXES, split_axis=0, concat_axis=0, tiled=True)  37.6 us
    pallas_call x1, Pallas kernels, body(): call(couple_kernel, 'couple', [square, (6 * ROWS, SEG)], 'ssvvvvvvvvv', [...  19.9 us
    pallas_call x1, Pallas kernels, body(): call(owner_kernel, 'owner', [nets, (2 * ROWS, SEG)], 'vhhhh', [(flat, F32...  8.76 us
    ppermute x1, starting transfers between devices, body(): far = lax.ppermute(far, AXES, between)  4.55 us
    pallas_call x1, Pallas kernels, body(): call(final_kernel, 'final', [square], 'vvv', [((2 * ROWS, CAPS), BF)], co...  3.26 us
    pallas_call x1, Pallas kernels, body(): rank, = call(rank_kernel, 'rank', [square], 'v', cost=3)(owner)  2.79 us
    ppermute x1, starting transfers between devices, body(): near = lax.ppermute(near, AXES, in_pair)  2.12 us
  transfers between devices with their start and end apart: 2, of which 0 were waited for; matrix products, arithmetic and copies ran while one was open for 0% of the time, Pallas kernels for 3%

profile of v4, /device:TPU:1, one launch (start us, length us, event | category | flops | bytes accessed | tf_op | source)
XLA Modules:
  0.0 81.3 jit_solution(16599684019402462701)
XLA Ops:
  0.6 0.0 copy-start.9
  0.6 1.5 %edge.1 = (f32[24,128]{1,0:T(8,128)}, f32[24,128]{1,0:T(8,128)}) custom-call(s32[1]{0:T(128)} %bitcast.first_ref, f32[128,128]{1,0:T(8,128)} %start_ref.1, f32[128,128]{1,0:T(8,128)} %len_ref.1, f32[128,128]{1,0:T(8,128)} %track_ref.1), custom_call_target="tpu_custom_call" | custom-call | tf_op jit(solution)/shard_map/edge/pallas_call | solution.py:392
  2.1 2.1 %collective-permute-start = (f32[24,128]{1,0:T(8,128)}, f32[24,128]{1,0:T(8,128)S(1)}, u32[]{:S(2)}, u32[]{:S(2)}) collective-permute-start(f32[24,128]{1,0:T(8,128)} %get-tuple-element.9), channel_id=1, source_target_pairs={{0,1},{1,0},{2,3},{3,2},{4,5},{5,4},{6,7},{7,6},{8,9},{9,8},{10,11... | collective-permute-start | bytes 36872 | tf_op jit(solution)/shard_map/ppermute | solution.py:395
  4.2 4.6 %collective-permute-start.1 = (f32[24,128]{1,0:T(8,128)}, f32[24,128]{1,0:T(8,128)S(1)}, u32[]{:S(2)}, u32[]{:S(2)}) collective-permute-start(f32[24,128]{1,0:T(8,128)} %get-tuple-element.10), channel_id=1, source_target_pairs={{1,2},{2,1},{3,4},{4,3},{5,6},{6,5},{7,8},{8,7},{9,10},{10,9},{11,... | collective-permute-start | bytes 36872 | tf_op jit(solution)/shard_map/ppermute | solution.py:394
  8.8 0.0 copy-done.9
  8.8 0.0 copy-start
  8.8 0.0 copy-start.1
  8.8 0.0 copy-start.2
  8.8 0.0 copy-start.3
  8.9 0.0 copy-start.4
  8.9 0.0 copy-start.10
  8.9 2.8 %rank.1.rank_ref = f32[128,128]{1,0:T(8,128)S(1)} custom-call(s32[128,128]{1,0:T(8,128)S(1)} %bitcast.11), custom_call_target="tpu_custom_call" | custom-call | flops 3000000000 | tf_op jit(solution)/shard_map/rank/pallas_call | solution.py:396
  11.7 0.0 collective-permute-done.near_ref
  11.7 0.0 collective-permute-done.1.far_ref
  11.7 0.0 copy-done
  11.7 0.0 copy-done.1
  11.7 0.0 copy-done.2
  11.7 0.0 copy-done.3
  11.8 19.9 %couple.1 = (f32[128,128]{1,0:T(8,128)}, f32[768,128]{1,0:T(8,128)S(1)}) custom-call(s32[1]{0:T(128)} %bitcast.first_ref, s32[4,128]{1,0:T(4,128)S(1)} %bitcast.14, f32[128,128]{1,0:T(8,128)S(1)} %copy-done, f32[128,128]{1,0:T(8,128)S(1)} %copy-done.1, f32[128,128]{1,0:T(8,128)S(1)} %copy-done.2, f32[24,128]{1,0:T(8,128)S(1)} %collective-permute-done.near_ref, ...), custom_call_target="tpu_custom_call" | custom-call | flops 20000000000 | tf_op jit(solution)/shard_map/couple/pallas_call | solution.py:398
  31.7 23.7 %all_to_all.10 = f32[128,1,768]{2,1,0:T(1,128)S(1)} all-to-all(f32[128,1,768]{2,1,0:T(1,128)S(1)} %bitcast.7), channel_id=1, replica_groups=mesh['tile'=32,'net'=4] {'tile','net'}, dimensions={0} | all-to-all | bytes 786432 | tf_op jit(solution)/shard_map/all_to_all | solution.py:380
  55.4 0.0 copy-done.7
  55.4 8.8 %owner.1 = (f32[32,512]{1,0:T(8,128)}, f32[256,128]{1,0:T(8,128)S(1)}) custom-call(f32[768,128]{1,0:T(8,128)S(1)} %bitcast.8, f32[32,512]{1,0:T(8,128)S(1)} %copy-done.5, f32[32,512]{1,0:T(8,128)S(1)} %copy-done.6, f32[32,512]{1,0:T(8,128)S(1)} %copy-done.7, s32[32,512]{1,0:T(8,128)S(1)} %copy-done.8), custom_call_target="tpu_custom_call" | custom-call | flops 8999999488 | tf_op jit(solution)/shard_map/owner/pallas_call | solution.py:404
  64.1 13.9 %all_to_all.11 = f32[128,1,256]{2,1,0:T(1,128)S(1)} all-to-all(f32[128,1,256]{2,1,0:T(1,128)S(1)} %bitcast.9), channel_id=1, replica_groups=mesh['tile'=32,'net'=4] {'tile','net'}, dimensions={0} | all-to-all | bytes 262144 | tf_op jit(solution)/shard_map/all_to_all | solution.py:380
  78.0 3.3 %final.1 = f32[128,128]{1,0:T(8,128)} custom-call(f32[256,128]{1,0:T(8,128)S(1)} %bitcast.10, s32[128,128]{1,0:T(8,128)S(1)} %bitcast.13, f32[128,128]{1,0:T(8,128)S(1)} %rank.1.rank_ref), custom_call_target="tpu_custom_call" | custom-call | flops 3000000000 | tf_op jit(solution)/shard_map/final/pallas_call | solution.py:410
  (9 shorter events, 0.0 us)
Async XLA Ops:
  0.6 8.2 %copy-start.9 = (s32[128,128,1]{1,2,0:T(1,128)S(1)}, s32[128,128,1]{1,2,0:T(1,128)}, u32[]{:S(2)}) copy-start(s32[128,128,1]{1,2,0:T(1,128)} %param.15) | copy-start | bytes 196612
  2.1 9.6 %collective-permute-start = (f32[24,128]{1,0:T(8,128)}, f32[24,128]{1,0:T(8,128)S(1)}, u32[]{:S(2)}, u32[]{:S(2)}) collective-permute-start(f32[24,128]{1,0:T(8,128)} %get-tuple-element.9), channel_id=1, source_target_pairs={{0,1},{1,0},{2,3},{3,2},{4,5},{5,4},{6,7},{7,6},{8,9},{9,8},{10,11... | collective-permute-start | bytes 36872 | tf_op jit(solution)/shard_map/ppermute | solution.py:395
  4.2 7.5 %collective-permute-start.1 = (f32[24,128]{1,0:T(8,128)}, f32[24,128]{1,0:T(8,128)S(1)}, u32[]{:S(2)}, u32[]{:S(2)}) collective-permute-start(f32[24,128]{1,0:T(8,128)} %get-tuple-element.10), channel_id=1, source_target_pairs={{1,2},{2,1},{3,4},{4,3},{5,6},{6,5},{7,8},{8,7},{9,10},{10,9},{11,... | collective-permute-start | bytes 36872 | tf_op jit(solution)/shard_map/ppermute | solution.py:394
  8.8 2.9 %copy-start = (f32[128,128]{1,0:T(8,128)S(1)}, f32[128,128]{1,0:T(8,128)}, u32[]{:S(2)}) copy-start(f32[128,128]{1,0:T(8,128)} %start_ref.1) | copy-start | bytes 196612
  8.8 2.9 %copy-start.1 = (f32[128,128]{1,0:T(8,128)S(1)}, f32[128,128]{1,0:T(8,128)}, u32[]{:S(2)}) copy-start(f32[128,128]{1,0:T(8,128)} %len_ref.1) | copy-start | bytes 196612
  8.8 2.9 %copy-start.2 = (f32[128,128]{1,0:T(8,128)S(1)}, f32[128,128]{1,0:T(8,128)}, u32[]{:S(2)}) copy-start(f32[128,128]{1,0:T(8,128)} %track_ref.1) | copy-start | bytes 196612
  8.8 2.9 %copy-start.3 = (s32[128,128]{1,0:T(8,128)S(1)}, s32[128,128]{1,0:T(8,128)}, u32[]{:S(2)}) copy-start(s32[128,128]{1,0:T(8,128)} %local_ref.1) | copy-start | bytes 196612
  8.9 2.9 %copy-start.4 = (s32[128,128]{1,0:T(8,128)S(1)}, s32[128,128]{1,0:T(8,128)}, u32[]{:S(2)}) copy-start(s32[128,128]{1,0:T(8,128)} %node_ref.1) | copy-start | bytes 196612
  8.9 2.9 %copy-start.10 = (s32[128,4]{0,1:T(4,128)S(1)}, s32[128,4]{0,1:T(4,128)}, u32[]{:S(2)}) copy-start(s32[128,4]{0,1:T(4,128)} %param.14) | copy-start | bytes 6148
  31.7 23.7 %copy-start.5 = (f32[32,512]{1,0:T(8,128)S(1)}, f32[32,512]{1,0:T(8,128)}, u32[]{:S(2)}) copy-start(f32[32,512]{1,0:T(8,128)} %pin_hbm.1) | copy-start | bytes 196612
  31.7 23.7 %copy-start.6 = (f32[32,512]{1,0:T(8,128)S(1)}, f32[32,512]{1,0:T(8,128)}, u32[]{:S(2)}) copy-start(f32[32,512]{1,0:T(8,128)} %load_hbm.1) | copy-start | bytes 196612
  31.7 23.7 %copy-start.7 = (f32[32,512]{1,0:T(8,128)S(1)}, f32[32,512]{1,0:T(8,128)}, u32[]{:S(2)}) copy-start(f32[32,512]{1,0:T(8,128)} %weight_hbm.1) | copy-start | bytes 196612
  31.7 23.7 %copy-start.8 = (s32[32,512]{1,0:T(8,128)S(1)}, s32[32,512]{1,0:T(8,128)}, u32[]{:S(2)}) copy-start(s32[32,512]{1,0:T(8,128)} %parent_hbm.1) | copy-start | bytes 196612

commit v5 on v4

--- a/solution.py
+++ b/solution.py
@@ -21,7 +21,7 @@
 VMEM_LIMIT = 24 * 1024 * 1024
 
 RANK_ROWS = 64
-COUPLE_STEPS = 2
+COUPLE_STEPS = 4
 OWNER_UNITS = 8
 FINAL_UNITS = 16
 
@@ -189,15 +189,18 @@
         power = jnp.exp2(((slot >> 7) - 63).astype(F32))
         return [cap_hi, cap_lo, res_hi, res_lo, power * (1.0 + (slot & 127).astype(F32) * (1.0 / 128))]
 
-    def send(j0, owner, rank, values):
-        cols = []
-        rows = []
+    def places(j0, rank):
+        return jnp.concatenate(
+            [jnp.where(iota_r == spread(rank[j:j + 1, :], CAPS), one, zero) for j in range(j0, j0 + 4)],
+            axis=1)
+
+    def send(j0, owner, right, values, low, high):
+        left = []
         for j in range(j0, j0 + 4):
             hit = iota_o == spread(owner[j:j + 1, :], ROWS)
-            cols.append(jnp.concatenate(
-                [jnp.where(hit, spread(v[j:j + 1, :], ROWS), zero) for v in values], axis=0))
-            rows.append(jnp.where(iota_r == spread(rank[j:j + 1, :], CAPS), one, zero))
-        acc[...] += mm(jnp.concatenate(cols, axis=1), jnp.concatenate(rows, axis=1), NT)
+            left.append(jnp.concatenate(
+                [jnp.where(hit, spread(v[j:j + 1, :], ROWS), zero) for v in values[low:high]], axis=0))
+        acc[low * ROWS:high * ROWS, :] += mm(jnp.concatenate(left, axis=1), right, NT)
 
     def step(g, full, full_next):
         turn(jnp.minimum(g + 1, ROWS // 8 - 1), full_next)
@@ -207,7 +210,10 @@
         sums = [jnp.zeros((8, SEG), F32)] * (SEG // 8)
         for j in range(8):
             if j % 4 == 0:
-                send(j, owner, rank, values)
+                right = places(j, rank)
+                send(j, owner, right, values, 0, 2)
+            if j % 4 == 2:
+                send(j - 2, owner, right, values, 2, 5)
             if j % 2 == 0:
                 wide = spread_pair(j // 2, full)
             pairs(g, j, wide, sums)
@@ -229,7 +235,7 @@
     last = ROWS // 8 - 1
     owner, rank, values = eight(owner_ref, last).astype(F32), eight(rank_ref, last), values_of(last)
     for j in range(0, 8, 4):
-        send(j, owner, rank, values)
+        send(j, owner, places(j, rank), values, 0, 5)
     for v in range(2):
         high = acc[2 * v * ROWS:(2 * v + 1) * ROWS, :]
         low = acc[(2 * v + 1) * ROWS:(2 * v + 2) * ROWS, :]

time: 81.5 us -> 79.8 us (0.979)
  Pallas kernels: 36.2 us -> 34.5 us
    pallas_call x1, Pallas kernels: 19.9 us -> 18.2 us  [body(): call(couple_kernel, 'couple', [square, (6 * ROWS, SEG)], 'ssvvvvvvvvv', [...]
where the time goes in v5:
time: 79.8 us; the launch traced here: 79.6 us
  blocking collectives  37.6 us (47%)
  Pallas kernels  34.5 us (43%)
  starting transfers between devices  6.67 us (8%)
  between operations  0.81 us (1%)
    all_to_all x2, blocking collectives, exchange(): lax.all_to_all(box, AXES, split_axis=0, concat_axis=0, tiled=True)  37.6 us
    pallas_call x1, Pallas kernels, body(): call(couple_kernel, 'couple', [square, (6 * ROWS, SEG)], 'ssvvvvvvvvv', [...  18.2 us
    pallas_call x1, Pallas kernels, body(): call(owner_kernel, 'owner', [nets, (2 * ROWS, SEG)], 'vhhhh', [(flat, F32...  8.76 us
    ppermute x1, starting transfers between devices, body(): far = lax.ppermute(far, AXES, between)  4.55 us
    pallas_call x1, Pallas kernels, body(): call(final_kernel, 'final', [square], 'vvv', [((2 * ROWS, CAPS), BF)], co...  3.26 us
    pallas_call x1, Pallas kernels, body(): rank, = call(rank_kernel, 'rank', [square], 'v', cost=3)(owner)  2.77 us
    ppermute x1, starting transfers between devices, body(): near = lax.ppermute(near, AXES, in_pair)  2.12 us
  transfers between devices with their start and end apart: 2, of which 0 were waited for; matrix products, arithmetic and copies ran while one was open for 0% of the time, Pallas kernels for 3%

profile of v5, /device:TPU:1, one launch (start us, length us, event | category | flops | bytes accessed | tf_op | source)
XLA Modules:
  0.0 79.6 jit_solution(12362177496801355550)
XLA Ops:
  0.6 1.5 %edge.1 = (f32[24,128]{1,0:T(8,128)}, f32[24,128]{1,0:T(8,128)}) custom-call(s32[1]{0:T(128)} %bitcast.first_ref, f32[128,128]{1,0:T(8,128)} %start_ref.1, f32[128,128]{1,0:T(8,128)} %len_ref.1, f32[128,128]{1,0:T(8,128)} %track_ref.1), custom_call_target="tpu_custom_call" | custom-call | tf_op jit(solution)/shard_map/edge/pallas_call | solution.py:398
  2.1 2.1 %collective-permute-start = (f32[24,128]{1,0:T(8,128)}, f32[24,128]{1,0:T(8,128)S(1)}, u32[]{:S(2)}, u32[]{:S(2)}) collective-permute-start(f32[24,128]{1,0:T(8,128)} %get-tuple-element.9), channel_id=1, source_target_pairs={{0,1},{1,0},{2,3},{3,2},{4,5},{5,4},{6,7},{7,6},{8,9},{9,8},{10,11... | collective-permute-start | bytes 36872 | tf_op jit(solution)/shard_map/ppermute | solution.py:401
  4.2 4.6 %collective-permute-start.1 = (f32[24,128]{1,0:T(8,128)}, f32[24,128]{1,0:T(8,128)S(1)}, u32[]{:S(2)}, u32[]{:S(2)}) collective-permute-start(f32[24,128]{1,0:T(8,128)} %get-tuple-element.10), channel_id=1, source_target_pairs={{1,2},{2,1},{3,4},{4,3},{5,6},{6,5},{7,8},{8,7},{9,10},{10,9},{11,... | collective-permute-start | bytes 36872 | tf_op jit(solution)/shard_map/ppermute | solution.py:400
  8.8 0.0 copy-start
  8.8 0.0 copy-start.1
  8.8 0.0 copy-start.2
  8.8 0.0 copy-start.3
  8.9 0.0 copy-start.4
  8.9 0.0 copy-start.10
  8.9 2.8 %rank.1.rank_ref = f32[128,128]{1,0:T(8,128)S(1)} custom-call(s32[128,128]{1,0:T(8,128)S(1)} %bitcast.11), custom_call_target="tpu_custom_call" | custom-call | flops 3000000000 | tf_op jit(solution)/shard_map/rank/pallas_call | solution.py:402
  11.7 0.0 collective-permute-done.near_ref
  11.7 0.0 collective-permute-done.1.far_ref
  11.7 0.0 copy-done
  11.7 0.0 copy-done.1
  11.7 0.0 copy-done.2
  11.7 0.0 copy-done.3
  11.7 0.0 copy-done.4
  11.7 0.0 copy-done.10
  11.7 18.2 %couple.1 = (f32[128,128]{1,0:T(8,128)}, f32[768,128]{1,0:T(8,128)S(1)}) custom-call(s32[1]{0:T(128)} %bitcast.first_ref, s32[4,128]{1,0:T(4,128)S(1)} %bitcast.14, f32[128,128]{1,0:T(8,128)S(1)} %copy-done, f32[128,128]{1,0:T(8,128)S(1)} %copy-done.1, f32[128,128]{1,0:T(8,128)S(1)} %copy-done.2, f32[24,128]{1,0:T(8,128)S(1)} %collective-permute-done.near_ref, ...), custom_call_target="tpu_custom_call" | custom-call | flops 20000000000 | tf_op jit(solution)/shard_map/couple/pallas_call | solution.py:404
  29.9 23.7 %all_to_all.10 = f32[128,1,768]{2,1,0:T(1,128)S(1)} all-to-all(f32[128,1,768]{2,1,0:T(1,128)S(1)} %bitcast.7), channel_id=1, replica_groups=mesh['tile'=32,'net'=4] {'tile','net'}, dimensions={0} | all-to-all | bytes 786432 | tf_op jit(solution)/shard_map/all_to_all | solution.py:386
  53.6 0.0 copy-done.5
  53.6 8.8 %owner.1 = (f32[32,512]{1,0:T(8,128)}, f32[256,128]{1,0:T(8,128)S(1)}) custom-call(f32[768,128]{1,0:T(8,128)S(1)} %bitcast.8, f32[32,512]{1,0:T(8,128)S(1)} %copy-done.5, f32[32,512]{1,0:T(8,128)S(1)} %copy-done.6, f32[32,512]{1,0:T(8,128)S(1)} %copy-done.7, s32[32,512]{1,0:T(8,128)S(1)} %copy-done.8), custom_call_target="tpu_custom_call" | custom-call | flops 8999999488 | tf_op jit(solution)/shard_map/owner/pallas_call | solution.py:410
  62.4 13.9 %all_to_all.11 = f32[128,1,256]{2,1,0:T(1,128)S(1)} all-to-all(f32[128,1,256]{2,1,0:T(1,128)S(1)} %bitcast.9), channel_id=1, replica_groups=mesh['tile'=32,'net'=4] {'tile','net'}, dimensions={0} | all-to-all | bytes 262144 | tf_op jit(solution)/shard_map/all_to_all | solution.py:386
  76.3 3.3 %final.1 = f32[128,128]{1,0:T(8,128)} custom-call(f32[256,128]{1,0:T(8,128)S(1)} %bitcast.10, s32[128,128]{1,0:T(8,128)S(1)} %bitcast.13, f32[128,128]{1,0:T(8,128)S(1)} %rank.1.rank_ref), custom_call_target="tpu_custom_call" | custom-call | flops 3000000000 | tf_op jit(solution)/shard_map/final/pallas_call | solution.py:416
  (9 shorter events, 0.0 us)
Async XLA Ops:
  0.6 8.2 %copy-start.9 = (s32[128,128,1]{1,2,0:T(1,128)S(1)}, s32[128,128,1]{1,2,0:T(1,128)}, u32[]{:S(2)}) copy-start(s32[128,128,1]{1,2,0:T(1,128)} %param.15) | copy-start | bytes 196612
  2.1 9.5 %collective-permute-start = (f32[24,128]{1,0:T(8,128)}, f32[24,128]{1,0:T(8,128)S(1)}, u32[]{:S(2)}, u32[]{:S(2)}) collective-permute-start(f32[24,128]{1,0:T(8,128)} %get-tuple-element.9), channel_id=1, source_target_pairs={{0,1},{1,0},{2,3},{3,2},{4,5},{5,4},{6,7},{7,6},{8,9},{9,8},{10,11... | collective-permute-start | bytes 36872 | tf_op jit(solution)/shard_map/ppermute | solution.py:401
  4.2 7.4 %collective-permute-start.1 = (f32[24,128]{1,0:T(8,128)}, f32[24,128]{1,0:T(8,128)S(1)}, u32[]{:S(2)}, u32[]{:S(2)}) collective-permute-start(f32[24,128]{1,0:T(8,128)} %get-tuple-element.10), channel_id=1, source_target_pairs={{1,2},{2,1},{3,4},{4,3},{5,6},{6,5},{7,8},{8,7},{9,10},{10,9},{11,... | collective-permute-start | bytes 36872 | tf_op jit(solution)/shard_map/ppermute | solution.py:400
  8.8 2.9 %copy-start = (f32[128,128]{1,0:T(8,128)S(1)}, f32[128,128]{1,0:T(8,128)}, u32[]{:S(2)}) copy-start(f32[128,128]{1,0:T(8,128)} %start_ref.1) | copy-start | bytes 196612
  8.8 2.9 %copy-start.1 = (f32[128,128]{1,0:T(8,128)S(1)}, f32[128,128]{1,0:T(8,128)}, u32[]{:S(2)}) copy-start(f32[128,128]{1,0:T(8,128)} %len_ref.1) | copy-start | bytes 196612
  8.8 2.9 %copy-start.2 = (f32[128,128]{1,0:T(8,128)S(1)}, f32[128,128]{1,0:T(8,128)}, u32[]{:S(2)}) copy-start(f32[128,128]{1,0:T(8,128)} %track_ref.1) | copy-start | bytes 196612
  8.8 2.9 %copy-start.3 = (s32[128,128]{1,0:T(8,128)S(1)}, s32[128,128]{1,0:T(8,128)}, u32[]{:S(2)}) copy-start(s32[128,128]{1,0:T(8,128)} %local_ref.1) | copy-start | bytes 196612
  8.9 2.9 %copy-start.4 = (s32[128,128]{1,0:T(8,128)S(1)}, s32[128,128]{1,0:T(8,128)}, u32[]{:S(2)}) copy-start(s32[128,128]{1,0:T(8,128)} %node_ref.1) | copy-start | bytes 196612
  8.9 2.9 %copy-start.10 = (s32[128,4]{0,1:T(4,128)S(1)}, s32[128,4]{0,1:T(4,128)}, u32[]{:S(2)}) copy-start(s32[128,4]{0,1:T(4,128)} %param.14) | copy-start | bytes 6148
  29.9 23.7 %copy-start.5 = (f32[32,512]{1,0:T(8,128)S(1)}, f32[32,512]{1,0:T(8,128)}, u32[]{:S(2)}) copy-start(f32[32,512]{1,0:T(8,128)} %pin_hbm.1) | copy-start | bytes 196612
  29.9 23.7 %copy-start.6 = (f32[32,512]{1,0:T(8,128)S(1)}, f32[32,512]{1,0:T(8,128)}, u32[]{:S(2)}) copy-start(f32[32,512]{1,0:T(8,128)} %load_hbm.1) | copy-start | bytes 196612
  29.9 23.7 %copy-start.7 = (f32[32,512]{1,0:T(8,128)S(1)}, f32[32,512]{1,0:T(8,128)}, u32[]{:S(2)}) copy-start(f32[32,512]{1,0:T(8,128)} %weight_hbm.1) | copy-start | bytes 196612
  29.9 23.7 %copy-start.8 = (s32[32,512]{1,0:T(8,128)S(1)}, s32[32,512]{1,0:T(8,128)}, u32[]{:S(2)}) copy-start(s32[32,512]{1,0:T(8,128)} %parent_hbm.1) | copy-start | bytes 196612

commit v6 on v5

--- a/solution.py
+++ b/solution.py
@@ -23,7 +23,7 @@
 RANK_ROWS = 64
 COUPLE_STEPS = 4
 OWNER_UNITS = 8
-FINAL_UNITS = 16
+FINAL_UNITS = 8
 
 NT = (((1,), (1,)), ((), ()))
 NN = (((1,), (0,)), ((), ()))
@@ -398,8 +398,9 @@
     near, far = call(edge_kernel, "edge", [(24, SEG)] * 2, "shhh", copies=6, limit=None)(
         first, seg_start, seg_len, seg_track)
     far = lax.ppermute(far, AXES, between)
+    rank, = call(rank_kernel, "rank", [square], "v", cost=3)(owner)
+    near, rank = lax.optimization_barrier((near, rank))
     near = lax.ppermute(near, AXES, in_pair)
-    rank, = call(rank_kernel, "rank", [square], "v", cost=3)(owner)
     wide = (ROWS + 16, SEG)
     seg_cap, outbox = call(
         couple_kernel, "couple", [square, (6 * ROWS, SEG)], "ssvvvvvvvvv",

time: 79.8 us -> 79.7 us (level)
  waiting for transfers between devices: 0.01 us -> 2.52 us
  blocking collectives: 37.6 us -> 35.7 us
  starting transfers between devices: 6.67 us -> 5.86 us
    ppermute x1, waiting for transfers between devices: 0.01 us -> 2.52 us  [body(): near = lax.ppermute(near, AXES, in_pair)]
    ppermute x1, starting transfers between devices: 2.12 us -> 0.09 us  [body(): near = lax.ppermute(near, AXES, in_pair)]
    all_to_all x2, blocking collectives: 37.6 us -> 35.7 us  [exchange(): lax.all_to_all(box, AXES, split_axis=0, concat_axis=0, tiled=True)]
    ppermute x1, starting transfers between devices: 4.55 us -> 5.78 us  [body(): far = lax.ppermute(far, AXES, between)]
  transfers between devices with their start and end apart: 2 -> 2, of which waited for: 0 -> 1; matrix products, arithmetic and copies ran while one was open for 0% -> 0% of each run, Pallas kernels for 3% -> 3%
where the time goes in v6:
time: 79.7 us; the launch traced here: 79.5 us
  blocking collectives  35.7 us (45%)
  Pallas kernels  34.5 us (43%)
  starting transfers between devices  5.86 us (7%)
  waiting for transfers between devices  2.52 us (3%)
  between operations  0.81 us (1%)
    all_to_all x2, blocking collectives, exchange(): lax.all_to_all(box, AXES, split_axis=0, concat_axis=0, tiled=True)  35.7 us
    pallas_call x1, Pallas kernels, body(): call(couple_kernel, 'couple', [square, (6 * ROWS, SEG)], 'ssvvvvvvvvv', [...  18.2 us
    pallas_call x1, Pallas kernels, body(): call(owner_kernel, 'owner', [nets, (2 * ROWS, SEG)], 'vhhhh', [(flat, F32...  8.77 us
    ppermute x1, starting transfers between devices, body(): far = lax.ppermute(far, AXES, between)  5.78 us
    pallas_call x1, Pallas kernels, body(): call(final_kernel, 'final', [square], 'vvv', [((2 * ROWS, CAPS), BF)], co...  3.29 us
    pallas_call x1, Pallas kernels, body(): rank, = call(rank_kernel, 'rank', [square], 'v', cost=3)(owner)  2.77 us
    ppermute x1, waiting for transfers between devices, body(): near = lax.ppermute(near, AXES, in_pair)  2.52 us
  transfers between devices with their start and end apart: 2, of which 1 were waited for; matrix products, arithmetic and copies ran while one was open for 0% of the time, Pallas kernels for 3%

profile of v6, /device:TPU:1, one launch (start us, length us, event | category | flops | bytes accessed | tf_op | source)
XLA Modules:
  0.0 79.5 jit_solution(5781257761020646046)
XLA Ops:
  0.6 0.0 copy-start.9
  0.6 1.5 %edge.1 = (f32[24,128]{1,0:T(8,128)}, f32[24,128]{1,0:T(8,128)}) custom-call(s32[1]{0:T(128)} %bitcast.first_ref, f32[128,128]{1,0:T(8,128)} %start_ref.1, f32[128,128]{1,0:T(8,128)} %len_ref.1, f32[128,128]{1,0:T(8,128)} %track_ref.1), custom_call_target="tpu_custom_call" | custom-call | tf_op jit(solution)/shard_map/edge/pallas_call | solution.py:398
  2.1 5.8 %collective-permute-start.1 = (f32[24,128]{1,0:T(8,128)}, f32[24,128]{1,0:T(8,128)S(1)}, u32[]{:S(2)}, u32[]{:S(2)}) collective-permute-start(f32[24,128]{1,0:T(8,128)} %get-tuple-element.13), channel_id=1, source_target_pairs={{1,2},{2,1},{3,4},{4,3},{5,6},{6,5},{7,8},{8,7},{9,10},{10,9},{11,... | collective-permute-start | bytes 36872 | tf_op jit(solution)/shard_map/ppermute | solution.py:400
  7.9 0.0 copy-done.9
  7.9 0.0 copy-start.11
  7.9 0.0 copy-start
  7.9 0.0 copy-start.1
  8.0 0.0 copy-start.2
  8.0 0.0 copy-start.3
  8.0 0.0 copy-start.4
  8.0 2.8 %rank.1.rank_ref = f32[128,128]{1,0:T(8,128)S(1)} custom-call(s32[128,128]{1,0:T(8,128)S(1)} %bitcast.11), custom_call_target="tpu_custom_call" | custom-call | flops 3000000000 | tf_op jit(solution)/shard_map/rank/pallas_call | solution.py:401
  10.8 0.0 copy-start.10
  10.8 0.0 copy-done.11
  10.8 0.1 collective-permute-start
  10.9 0.0 collective-permute-done.1.far_ref
  10.9 2.5 %collective-permute-done.near_ref = f32[24,128]{1,0:T(8,128)S(1)} collective-permute-done((f32[24,128]{1,0:T(8,128)S(1)}, f32[24,128]{1,0:T(8,128)S(1)}, u32[]{:S(2)}, u32[]{:S(2)}) %collective-permute-start) | collective-permute-done | bytes 12320 | tf_op jit(solution)/shard_map/ppermute | solution.py:403
  13.4 0.0 copy-done
  13.4 0.0 copy-done.2
  13.5 18.2 %couple.1 = (f32[128,128]{1,0:T(8,128)}, f32[768,128]{1,0:T(8,128)S(1)}) custom-call(s32[1]{0:T(128)} %bitcast.first_ref, s32[4,128]{1,0:T(4,128)S(1)} %bitcast.14, f32[128,128]{1,0:T(8,128)S(1)} %copy-done, f32[128,128]{1,0:T(8,128)S(1)} %copy-done.1, f32[128,128]{1,0:T(8,128)S(1)} %copy-done.2, f32[24,128]{1,0:T(8,128)S(1)} %collective-permute-done.near_ref, ...), custom_call_target="tpu_custom_call" | custom-call | flops 20000000000 | tf_op jit(solution)/shard_map/couple/pallas_call | solution.py:405
  31.7 21.9 %all_to_all.10 = f32[128,1,768]{2,1,0:T(1,128)S(1)} all-to-all(f32[128,1,768]{2,1,0:T(1,128)S(1)} %bitcast.7), channel_id=1, replica_groups=mesh['tile'=32,'net'=4] {'tile','net'}, dimensions={0} | all-to-all | bytes 786432 | tf_op jit(solution)/shard_map/all_to_all | solution.py:386
  53.5 0.0 copy-done.6
  53.5 8.8 %owner.1 = (f32[32,512]{1,0:T(8,128)}, f32[256,128]{1,0:T(8,128)S(1)}) custom-call(f32[768,128]{1,0:T(8,128)S(1)} %bitcast.8, f32[32,512]{1,0:T(8,128)S(1)} %copy-done.5, f32[32,512]{1,0:T(8,128)S(1)} %copy-done.6, f32[32,512]{1,0:T(8,128)S(1)} %copy-done.7, s32[32,512]{1,0:T(8,128)S(1)} %copy-done.8), custom_call_target="tpu_custom_call" | custom-call | flops 8999999488 | tf_op jit(solution)/shard_map/owner/pallas_call | solution.py:411
  62.3 13.9 %all_to_all.11 = f32[128,1,256]{2,1,0:T(1,128)S(1)} all-to-all(f32[128,1,256]{2,1,0:T(1,128)S(1)} %bitcast.9), channel_id=1, replica_groups=mesh['tile'=32,'net'=4] {'tile','net'}, dimensions={0} | all-to-all | bytes 262144 | tf_op jit(solution)/shard_map/all_to_all | solution.py:386
  76.2 3.3 %final.1 = f32[128,128]{1,0:T(8,128)} custom-call(f32[256,128]{1,0:T(8,128)S(1)} %bitcast.10, s32[128,128]{1,0:T(8,128)S(1)} %bitcast.13, f32[128,128]{1,0:T(8,128)S(1)} %rank.1.rank_ref), custom_call_target="tpu_custom_call" | custom-call | flops 3000000000 | tf_op jit(solution)/shard_map/final/pallas_call | solution.py:417
  (11 shorter events, 0.0 us)
Async XLA Ops:
  0.6 7.3 %copy-start.9 = (s32[128,128,1]{1,2,0:T(1,128)S(1)}, s32[128,128,1]{1,2,0:T(1,128)}, u32[]{:S(2)}) copy-start(s32[128,128,1]{1,2,0:T(1,128)} %param.15) | copy-start | bytes 196612
  2.1 8.8 %collective-permute-start.1 = (f32[24,128]{1,0:T(8,128)}, f32[24,128]{1,0:T(8,128)S(1)}, u32[]{:S(2)}, u32[]{:S(2)}) collective-permute-start(f32[24,128]{1,0:T(8,128)} %get-tuple-element.13), channel_id=1, source_target_pairs={{1,2},{2,1},{3,4},{4,3},{5,6},{6,5},{7,8},{8,7},{9,10},{10,9},{11,... | collective-permute-start | bytes 36872 | tf_op jit(solution)/shard_map/ppermute | solution.py:400
  7.9 2.9 %copy-start.11 = (f32[24,128]{1,0:T(8,128)S(1)}, f32[24,128]{1,0:T(8,128)}, u32[]{:S(2)}) copy-start(f32[24,128]{1,0:T(8,128)} %get-tuple-element.12) | copy-start | bytes 36868
  7.9 5.5 %copy-start = (f32[128,128]{1,0:T(8,128)S(1)}, f32[128,128]{1,0:T(8,128)}, u32[]{:S(2)}) copy-start(f32[128,128]{1,0:T(8,128)} %start_ref.1) | copy-start | bytes 196612
  7.9 5.5 %copy-start.1 = (f32[128,128]{1,0:T(8,128)S(1)}, f32[128,128]{1,0:T(8,128)}, u32[]{:S(2)}) copy-start(f32[128,128]{1,0:T(8,128)} %len_ref.1) | copy-start | bytes 196612
  8.0 5.5 %copy-start.2 = (f32[128,128]{1,0:T(8,128)S(1)}, f32[128,128]{1,0:T(8,128)}, u32[]{:S(2)}) copy-start(f32[128,128]{1,0:T(8,128)} %track_ref.1) | copy-start | bytes 196612
  8.0 5.5 %copy-start.3 = (s32[128,128]{1,0:T(8,128)S(1)}, s32[128,128]{1,0:T(8,128)}, u32[]{:S(2)}) copy-start(s32[128,128]{1,0:T(8,128)} %local_ref.1) | copy-start | bytes 196612
  8.0 5.5 %copy-start.4 = (s32[128,128]{1,0:T(8,128)S(1)}, s32[128,128]{1,0:T(8,128)}, u32[]{:S(2)}) copy-start(s32[128,128]{1,0:T(8,128)} %node_ref.1) | copy-start | bytes 196612
  10.8 2.7 %copy-start.10 = (s32[128,4]{0,1:T(4,128)S(1)}, s32[128,4]{0,1:T(4,128)}, u32[]{:S(2)}) copy-start(s32[128,4]{0,1:T(4,128)} %param.14) | copy-start | bytes 6148
  10.8 2.6 %collective-permute-start = (f32[24,128]{1,0:T(8,128)S(1)}, f32[24,128]{1,0:T(8,128)S(1)}, u32[]{:S(2)}, u32[]{:S(2)}) collective-permute-start(f32[24,128]{1,0:T(8,128)S(1)} %copy-done.11), channel_id=1, source_target_pairs={{0,1},{1,0},{2,3},{3,2},{4,5},{5,4},{6,7},{7,6},{8,9},{9,8},{10,11... | collective-permute-start | bytes 36872 | tf_op jit(solution)/shard_map/ppermute | solution.py:403
  31.6 21.9 %copy-start.5 = (f32[32,512]{1,0:T(8,128)S(1)}, f32[32,512]{1,0:T(8,128)}, u32[]{:S(2)}) copy-start(f32[32,512]{1,0:T(8,128)} %pin_hbm.1) | copy-start | bytes 196612
  31.6 21.9 %copy-start.6 = (f32[32,512]{1,0:T(8,128)S(1)}, f32[32,512]{1,0:T(8,128)}, u32[]{:S(2)}) copy-start(f32[32,512]{1,0:T(8,128)} %load_hbm.1) | copy-start | bytes 196612
  31.6 21.9 %copy-start.7 = (f32[32,512]{1,0:T(8,128)S(1)}, f32[32,512]{1,0:T(8,128)}, u32[]{:S(2)}) copy-start(f32[32,512]{1,0:T(8,128)} %weight_hbm.1) | copy-start | bytes 196612
  31.6 21.9 %copy-start.8 = (s32[32,512]{1,0:T(8,128)S(1)}, s32[32,512]{1,0:T(8,128)}, u32[]{:S(2)}) copy-start(s32[32,512]{1,0:T(8,128)} %parent_hbm.1) | copy-start | bytes 196612
